TPU v7x, 32 devices: a whole 2x2x4 slice. The times are simulated.
32 devices in a mesh: groups: 2 (over y), blocks: 4 (over z), halo: 2 (over x), gz: 2 (over core).
Axes of the slice: x: 2, y: 2, z: 4, core: 2. Of those that a mesh axis runs over, the one named last changes fastest.
Arguments:
- raw_volume: bfloat16 [256, 16, 128], P(('groups', 'blocks', 'gz'), 'halo'), parts along dimension 0, may hold values from -6 to 6
- tissue_counts: int32 [16, 2, 4], P(('groups', 'blocks', 'gz'), 'halo'), parts along dimension 0, may hold values from 0 to 8192, as said below
- patch_core_offsets: int32 [16, 2, 4], P(('groups', 'blocks', 'gz'), 'halo'), parts along dimension 0, may hold values from 0 to 8
- w_first: bfloat16 [64, 1, 3, 3, 3], replicated, may hold values from -1.25 to 1.25
- w_second: bfloat16 [27, 4096], replicated, may hold values from -0.15625 to 0.15625
- w_coarse: bfloat16 [27, 4096], replicated, may hold values from -0.15625 to 0.15625
- w_head: bfloat16 [3, 64], replicated, may hold values from -0.75 to 0.75
Outputs:
- affinities: float32 [3, 256, 16, 128], P(None, ('groups', 'blocks', 'gz'), 'halo'), parts along dimension 1
There are 2 independent parts, one for each index of `groups`. A program takes and returns all parts, laid end to end along the dimension named above; an argument that names none is the same for every part. Nothing has to cross between parts.
Inputs may be any that keep to these rules, and one draw needn't show every extreme that they name: `tissue_counts`: in every group of 4 tiles that share their index along gz and their index h, exactly 4 slots are dense; a tile has at most 3 dense slots, and some tile of every such group has exactly 3.
All inputs are finite; a program needn't handle non-finite values.
Results may differ from a plain program's by a relative error of at most 0.004.
Values may be sent and summed in bfloat16 or wider, within the bound.
No kernel may reach another device: no remote copies, remote signals or barrier semaphores. Data moves between devices by JAX's collectives and lax.ppermute only.
A program may use at most 64 MiB of HBM per device.

v0:
```python
import jax
import jax.numpy as jnp
from jax import lax
from jax.sharding import PartitionSpec as P

PATCH_CORE_DEPTH = 8
WORK = 1
MOST = 3
MINC = 4096


conv_dims = ("NCDHW", "OIDHW", "NCDHW")


def padded(cells, sides, width):
    for axis, dim in sides:
        count = lax.axis_size(axis)
        ends = count - 1
        head = lax.slice_in_dim(cells, 0, width, axis=dim)
        tail = lax.slice_in_dim(cells, cells.shape[dim] - width, cells.shape[dim], axis=dim)
        cells = jnp.concatenate(
            [
                lax.ppermute(tail, axis, [(i, (i + 1) % count) for i in range(ends)]),
                cells,
                lax.ppermute(head, axis, [((i + 1) % count, i) for i in range(ends)]),
            ],
            axis=dim,
        )
    return cells


def shortened(array):

    def short(part):
        return part.astype(jnp.bfloat16) if part.dtype == jnp.float32 else part

    return jax.tree.map(short, array)


def as_kernel(flat_weight, channels):
    return jnp.transpose(flat_weight.reshape(3, 3, 3, channels, channels), (3, 4, 0, 1, 2))


def convolve(inputs, kernel):
    result = lax.conv_general_dilated(
        inputs,
        kernel,
        (1, 1, 1),
        ((0, 0), (0, 0), (1, 1)),
        dimension_numbers=conv_dims,
        preferred_element_type=jnp.float32,
    )
    return jnp.maximum(result, 0.0).astype(jnp.bfloat16)


def unet_level(window, w_first, w_second, w_coarse, w_head):
    channels = w_head.shape[1]
    batched = window[None, None]
    first_act = convolve(batched, w_first)
    second_act = convolve(first_act, as_kernel(w_second, channels))
    depth, rows, cells = (second_act.shape[2], second_act.shape[3], second_act.shape[4])
    pooled = second_act.astype(jnp.float32).reshape(
        1, channels, depth // 2, 2, rows // 2, 2, cells // 2, 2
    )
    pooled = jnp.mean(pooled, axis=(3, 5, 7)).astype(jnp.bfloat16)
    coarse = convolve(pooled, as_kernel(w_coarse, channels))
    upsampled = jnp.repeat(jnp.repeat(jnp.repeat(coarse, 2, axis=2), 2, axis=3), 2, axis=4)
    cropped = second_act[:, :, 2 : depth - 2, 2 : rows - 2, :]
    merged = (upsampled.astype(jnp.float32) + cropped.astype(jnp.float32)).astype(jnp.bfloat16)
    logits = jnp.einsum("oc,czyx->ozyx", w_head, merged[0], preferred_element_type=jnp.float32)
    return jax.nn.sigmoid(logits).astype(jnp.bfloat16)


def rank_tables(flags, owner_index, block_count, slot_count):
    flat_flags = flags.reshape(-1)
    global_rank = (jnp.cumsum(flat_flags) - flat_flags).reshape(block_count, slot_count)
    my_rank = lax.dynamic_index_in_dim(global_rank, owner_index, 0, keepdims=False)
    per_block = jnp.sum(flags, axis=1)
    block_ends = jnp.cumsum(per_block)
    block_starts = block_ends - per_block
    wanted = owner_index * WORK + jnp.arange(WORK)
    source_block = jnp.sum((block_ends[None, :] <= wanted[:, None]).astype(jnp.int32), axis=1)
    source_block = jnp.minimum(source_block, block_count - 1)
    local_index = jnp.clip(wanted - block_starts[source_block], 0, MOST - 1)
    return (my_rank, source_block, local_index)


def local(raw_volume, tissue_counts, patch_core_offsets, w_first, w_second, w_coarse, w_head):
    extended = padded(raw_volume, ((("blocks", "gz"), 0), ("halo", 1)), 4)
    tile_depth = raw_volume.shape[0]
    window_rows = extended.shape[1]
    x_cells = extended.shape[2]
    counts_here = tissue_counts[0, 0]
    anchors_here = patch_core_offsets[0, 0]
    slot_count = counts_here.shape[0]
    active_here = (counts_here >= MINC).astype(jnp.int32)
    zero_index = jnp.int32(0)
    local_rank = jnp.cumsum(active_here) - active_here
    block_count = lax.axis_size("blocks")
    owner_index = lax.axis_index("blocks")
    everyone = lax.all_gather(tissue_counts, "blocks", axis=0, tiled=True)
    flags = (everyone[:, 0, :] >= MINC).astype(jnp.int32)
    my_rank, source_block, local_index = rank_tables(flags, owner_index, block_count, slot_count)

    def cut_window(anchor):
        return lax.dynamic_slice(
            extended, (anchor, zero_index, zero_index), (PATCH_CORE_DEPTH + 8, window_rows, x_cells)
        )

    windows = jax.vmap(cut_window)(anchors_here)
    selector = (active_here[None, :] == 1) & (local_rank[None, :] == jnp.arange(MOST)[:, None])
    gathered = lax.all_gather(
        jnp.einsum(
            "ks,szyx->kzyx",
            selector.astype(jnp.bfloat16),
            windows,
            preferred_element_type=jnp.float32,
        ).astype(jnp.bfloat16),
        "blocks",
        axis=0,
        tiled=True,
    )
    work_items = gathered[source_block * MOST + local_index]
    predicted = lax.map(
        lambda window: unet_level(window, w_first, w_second, w_coarse, w_head), work_items
    )
    arrived = jax.tree.map(
        lambda part, own: part.astype(own.dtype),
        lax.all_gather(shortened(predicted), "blocks", axis=0, tiled=True),
        predicted,
    )
    own_preds = arrived[jnp.minimum(my_rank, block_count * WORK - 1)]
    depth_pos = jnp.arange(PATCH_CORE_DEPTH).astype(jnp.float32)
    blend_weight = (depth_pos + 1.0) * (PATCH_CORE_DEPTH - depth_pos)
    blend_weight = blend_weight / jnp.max(blend_weight)
    landing = (
        jnp.arange(tile_depth)[None, None, :]
        == anchors_here[:, None, None] + jnp.arange(PATCH_CORE_DEPTH)[None, :, None]
    )
    placement = (
        active_here[:, None, None].astype(jnp.float32)
        * landing.astype(jnp.float32)
        * blend_weight[None, :, None]
    )
    numerator = jnp.einsum(
        "stz,sctyx->czyx", placement, own_preds.astype(jnp.float32), precision=lax.Precision.HIGHEST
    )
    coverage = jnp.sum(placement, axis=(0, 1))
    return numerator / jnp.maximum(coverage, 1.0)[None, :, None, None]


def solution(mesh):
    in_specs = (
        P(("groups", "blocks", "gz"), "halo", None),
        P(("groups", "blocks", "gz"), "halo", None),
        P(("groups", "blocks", "gz"), "halo", None),
        P(),
        P(),
        P(),
        P(),
    )
    out_specs = P(None, ("groups", "blocks", "gz"), "halo", None)
    return jax.shard_map(local, mesh=mesh, in_specs=in_specs, out_specs=out_specs, check_vma=False)
```

profile of v0, /device:TPU:0, one launch (start us, length us, event | category | flops | bytes accessed | tf_op | source)
XLA Modules:
  0.0 172.8 jit_solution(17559018112930659023)
XLA Ops:
  0.0 0.7 fusion.91
  0.7 1.3 collective-permute-start.1
  2.0 3.0 %collective-permute-start = (bf16[4,8,128]{2,1,0:T(8,128)(2,1)S(1)}, bf16[4,8,128]{2,1,0:T(8,128)(2,1)S(1)}, u32[]{:S(2)}, u32[]{:S(2)}) collective-permute-start(bf16[4,8,128]{2,1,0:T(8,128)(2,1)S(1)} %get-tuple-element.55), channel_id=1, source_target_pairs={{0,1},{1,4},{4,5},{5,8},{8,9},{9,12},{12,13},{2,3},{3,6},{6,7},{7,... | collective-permute-start | bytes 24584 | tf_op jit(solution)/shard_map/ppermute | solution.py:23
  5.1 0.7 fusion.77
  5.7 0.7 bitcast_compare_fusion
  6.4 0.7 bitcast_convert_fusion
  7.1 12.7 %all_gather.10 = s32[4,1,4]{2,1,0:T(1,128)S(1)} all-gather(s32[1,1,4]{2,1,0:T(1,128)} %param.8), channel_id=1, replica_groups=mesh['groups'=2,'blocks'=4,'halo'=2,'gz'=2] {'blocks'}, dimensions={0}, use_global_device_ids=true | all-gather | bytes 80 | tf_op jit(solution)/shard_map/all_gather | solution.py:101
  19.8 0.2 fusion.87
  19.9 0.7 broadcast_divide_fusion
  20.6 0.7 fusion.75
  21.3 0.2 reduce-window.18
  21.5 0.7 bitcast_subtract_fusion.1
  22.1 0.7 iota_add_fusion
  23.0 0.2 reduce-window.19
  23.5 0.8 constant_dynamic-update-slice_fusion.1
  24.3 3.4 %collective-permute-start.2 = (bf16[24,4,128]{2,1,0:T(4,128)(2,1)S(1)}, bf16[24,4,128]{2,1,0:T(4,128)(2,1)S(1)}, u32[]{:S(2)}, u32[]{:S(2)}) collective-permute-start(bf16[24,4,128]{2,1,0:T(4,128)(2,1)S(1)} %get-tuple-element.52), channel_id=1, source_target_pairs={{0,2},{1,3},{4,6},{5,7},{8,10},{9,11},{12,14},{13,15},{16,18},{17,... | collective-permute-start | bytes 73736 | tf_op jit(solution)/shard_map/ppermute | solution.py:23
  27.7 1.3 collective-permute-start.3
  29.0 0.6 fusion.72
  30.2 0.6 dynamic-slice.5
  31.4 2.2 %reshape.281 = bf16[3,3,3,64,64]{4,3,2,1,0:T(8,128)(2,1)} reshape(bf16[27,4096]{1,0:T(8,128)(2,1)} %param.11) | data formatting | bytes 442368 | tf_op jit(solution)/shard_map/while/body/eval_jaxpr/reshape | solution.py:41
  33.6 1.4 reshape.284
  35.1 0.6 gather_fusion
  35.7 0.3 convolution_convert_fusion
  36.1 16.3 %all_gather.9 = bf16[12,16,16,128]{3,2,1,0:T(8,128)(2,1)S(1)} all-gather(bf16[3,16,16,128]{3,2,1,0:T(8,128)(2,1)S(1)} %copy.26), channel_id=1, replica_groups=mesh['groups'=2,'blocks'=4,'halo'=2,'gz'=2] {'blocks'}, dimensions={0}, use_global_device_ids=true | all-gather | bytes 983040 | tf_op jit(solution)/shard_map/all_gather | solution.py:112
  52.5 0.4 reshape.331
  53.0 0.4 fusion.55
  53.4 4.0 %copy.27 = bf16[1,16,16,8,19]{3,0,4,2,1:T(2,128)(2,1)S(1)} copy(bf16[1,16,16,8,19]{4,3,2,1,0:T(8,128)(2,1)S(1)} %fusion.55) | data formatting | bytes 155648 | tf_op jit(solution)/shard_map/while/body/eval_jaxpr/conv_general_dilated | solution.py:45
  57.4 23.2 %fusion.14 = bf16[14,14,1,8,17,64]{5,3,4,1,0,2:T(8,128)(2,1)S(1)} fusion(bf16[1,16,16,8,19]{3,0,4,2,1:T(2,128)(2,1)S(1)} %copy.27, pred[8,17]{0,1:T(8,128)(4,1)S(1)} %copy-done.3, bf16[64,1,3,3,3]{0,4,3,2,1:T(4,128)(2,1)S(1)} %copy-done), kind=kOutput, calls=%fused_computation.18 | convolution fusion | flops 98947072 | bytes 3493384 | tf_op jit(solution)/shard_map/while/body/eval_jaxpr/conv_general_dilated | solution.py:45
  80.6 0.2 fusion.89
  80.8 36.0 %maximum_convert_fusion.1 = bf16[12,12,8,17,64]{4,2,3,1,0:T(8,128)(2,1)S(1)} fusion(bf16[3,3,3,64,64]{4,3,2,1,0:T(8,128)(2,1)S(1)} %copy-done.1, bf16[14,14,1,7,1,64]{5,3,4,1,0,2:T(8,128)(2,1)S(1)} %get-tuple-element.51, bf16[14,14,1,7,1,64]{5,3,4,1,0,2:T(8,128)(2,1)S(1)} %get-tuple-element.50, bf16[14,14,1,8,17,64]{5,3,4,1,0,2:T(8,128)(2,1)S(1)} %fusion.14), kind=kOutput, calls=%fused_computation.7 | convolution fusion | flops 4353241088 | bytes 6491136 | tf_op jit(solution)/shard_map/while/body/eval_jaxpr/conv_general_dilated | solution.py:45
  116.8 0.3 slice_convert_fusion.1
  117.1 5.1 %copy.29 = bf16[12,12,8,17,64]{4,3,2,1,0:T(8,128)(2,1)} copy(bf16[12,12,8,17,64]{4,2,3,1,0:T(8,128)(2,1)S(1)} %maximum_convert_fusion.1) | data formatting | bytes 5013504 | tf_op jit(solution)/shard_map/while/body/eval_jaxpr/convert_element_type | solution.py:53
  122.2 2.8 %copy.34 = f32[8,8,8,17,64]{4,1,3,2,0:T(8,128)} copy(f32[8,8,8,17,64]{4,2,3,1,0:T(8,128)S(1)} %slice_convert_fusion.1) | data formatting | bytes 4456448 | tf_op jit(solution)/shard_map/while/body/eval_jaxpr/convert_element_type | solution.py:69
  125.1 9.8 %reshape.338 = bf16[12,12,1,136,64]{4,3,1,0,2:T(8,128)(2,1)} reshape(bf16[12,12,8,17,64]{4,3,2,1,0:T(8,128)(2,1)} %copy.29) | data formatting | bytes 5013504 | tf_op jit(solution)/shard_map/while/body/eval_jaxpr/convert_element_type | solution.py:53
  134.9 7.2 %slice_convert_fusion = f32[12,12,1,128,64]{4,3,1,0,2:T(8,128)} fusion(bf16[12,12,1,136,64]{4,3,1,0,2:T(8,128)(2,1)} %reshape.338), kind=kLoop, calls=%fused_computation.19 | loop fusion | flops 1179648 | bytes 7077888 | tf_op jit(solution)/shard_map/while/body/eval_jaxpr/reshape | solution.py:62
  142.1 9.5 %reduce_sum.39 = f32[64,6,6,64]{0,3,2,1:T(8,128)S(1)} reduce(f32[64,6,2,6,2,64,2]{0,6,5,4,3,2,1:T(2,128)} %bitcast.98, f32[]{:T(128)} %constant.47.clone.1), dimensions={2,4,6}, to_apply=%region_4.5 | reduce | flops 1032192 | bytes 5308420 | tf_op jit(solution)/shard_map/while/body/eval_jaxpr/reduce_sum | solution.py:65
  151.7 0.4 copy.44
  152.1 0.2 pad.9.clone
  152.5 2.2 %fusion.25 = bf16[4,4,8,9,64]{4,2,3,1,0:T(8,128)(2,1)S(1)} fusion(bf16[3,3,3,64,64]{4,3,2,1,0:T(8,128)(2,1)S(1)} %reshape.284, bf16[64,6,6,1,7,2]{0,4,5,2,1,3:T(8,128)(2,1)S(1)} %slice.56, bf16[64,6,6,1,8,9]{0,4,5,2,1,3:T(8,128)(2,1)S(1)} %copy.32, pred[8,9]{0,1:T(8,128)(4,1)S(1)} %copy-done.4), kind=kOutput, calls=%fused_computation.32 | convolution fusion | flops 256241664 | bytes 765000 | tf_op jit(solution)/shard_map/while/body/eval_jaxpr/conv_general_dilated | solution.py:45
  155.1 0.7 broadcast_in_dim.43
  155.8 0.3 broadcast_in_dim.44
  156.1 0.4 fusion.20
  156.5 0.3 copy-done.2
  156.8 0.7 fusion.41
  157.5 13.6 %all-gather = bf16[12,8,8,128]{3,2,1,0:T(8,128)(2,1)S(1)} all-gather(bf16[3,8,8,128]{3,2,1,0:T(8,128)(2,1)S(1)} %copy.36), channel_id=2, replica_groups=mesh['groups'=2,'blocks'=4,'halo'=2,'gz'=2] {'blocks'}, dimensions={0}, use_global_device_ids=true | all-gather | bytes 245760 | tf_op jit(solution)/shard_map/all_gather | solution.py:129
  171.1 0.6 gather_fusion.1
  171.6 0.4 fusion.45
  172.0 0.7 copy.39
  (44 shorter events, 1.4 us)
Async XLA Ops:
  0.0 57.4 %copy-start = (bf16[64,1,3,3,3]{0,4,3,2,1:T(4,128)(2,1)S(1)}, bf16[64,1,3,3,3]{0,4,3,2,1:T(4,128)(2,1)}, u32[]{:S(2)}) copy-start(bf16[64,1,3,3,3]{0,4,3,2,1:T(4,128)(2,1)} %param.10) | copy-start | bytes 10372
  0.7 23.6 %collective-permute-start.1 = (bf16[4,8,128]{2,1,0:T(8,128)(2,1)S(1)}, bf16[4,8,128]{2,1,0:T(8,128)(2,1)S(1)}, u32[]{:S(2)}, u32[]{:S(2)}) collective-permute-start(bf16[4,8,128]{2,1,0:T(8,128)(2,1)S(1)} %get-tuple-element.54), channel_id=1, source_target_pairs={{1,0},{4,1},{5,4},{8,5},{9,8},{12,9},{13,12},{3,2},{6,3},{7,6},{10... | collective-permute-start | bytes 24584 | tf_op jit(solution)/shard_map/ppermute | solution.py:25
  2.0 21.5 %collective-permute-start = (bf16[4,8,128]{2,1,0:T(8,128)(2,1)S(1)}, bf16[4,8,128]{2,1,0:T(8,128)(2,1)S(1)}, u32[]{:S(2)}, u32[]{:S(2)}) collective-permute-start(bf16[4,8,128]{2,1,0:T(8,128)(2,1)S(1)} %get-tuple-element.55), channel_id=1, source_target_pairs={{0,1},{1,4},{4,5},{5,8},{8,9},{9,12},{12,13},{2,3},{3,6},{6,7},{7,... | collective-permute-start | bytes 24584 | tf_op jit(solution)/shard_map/ppermute | solution.py:23
  24.3 10.7 %collective-permute-start.2 = (bf16[24,4,128]{2,1,0:T(4,128)(2,1)S(1)}, bf16[24,4,128]{2,1,0:T(4,128)(2,1)S(1)}, u32[]{:S(2)}, u32[]{:S(2)}) collective-permute-start(bf16[24,4,128]{2,1,0:T(4,128)(2,1)S(1)} %get-tuple-element.52), channel_id=1, source_target_pairs={{0,2},{1,3},{4,6},{5,7},{8,10},{9,11},{12,14},{13,15},{16,18},{17,... | collective-permute-start | bytes 73736 | tf_op jit(solution)/shard_map/ppermute | solution.py:23
  27.7 7.3 %collective-permute-start.3 = (bf16[24,4,128]{2,1,0:T(4,128)(2,1)S(1)}, bf16[24,4,128]{2,1,0:T(4,128)(2,1)S(1)}, u32[]{:S(2)}, u32[]{:S(2)}) collective-permute-start(bf16[24,4,128]{2,1,0:T(4,128)(2,1)S(1)} %get-tuple-element.53), channel_id=1, source_target_pairs={{2,0},{3,1},{6,4},{7,5},{10,8},{11,9},{14,12},{15,13},{18,16},{19,... | collective-permute-start | bytes 73736 | tf_op jit(solution)/shard_map/ppermute | solution.py:25
  33.6 23.8 %copy-start.3 = (pred[8,17]{0,1:T(8,128)(4,1)S(1)}, pred[8,17]{0,1:T(8,128)(4,1)}, u32[]{:S(2)}) copy-start(pred[8,17]{0,1:T(8,128)(4,1)} %constant.127) | copy-start | bytes 412
  57.4 23.4 %copy-start.1 = (bf16[3,3,3,64,64]{4,3,2,1,0:T(8,128)(2,1)S(1)}, bf16[3,3,3,64,64]{4,3,2,1,0:T(8,128)(2,1)}, u32[]{:S(2)}) copy-start(bf16[3,3,3,64,64]{4,3,2,1,0:T(8,128)(2,1)} %reshape.281) | copy-start | bytes 663556
  151.6 0.9 copy-start.4
  152.5 3.6 %slice-start = ((s8[4456448]{0:T(1024)(128)(4,1)}), s8[4194304]{0:T(1024)(128)(4,1)S(1)}, s32[]{:S(2)}) async-start(s8[4456448]{0:T(1024)(128)(4,1)} %bitcast.99), calls=%async_computation | async-start | bytes 8388608
  154.9 1.2 slice-start.1
  156.1 0.7 copy-start.2
where the time goes:
time: 174 us; the launch traced here: 173 us
  matrix products  62.7 us (36%)
  blocking collectives  42.6 us (24%)
  local copies, waits for them, and re-layouts  32.7 us (19%)
  other arithmetic  24.2 us (14%)
  starting transfers between devices  9 us (5%)
    conv_general_dilated x3, matrix products, convolve(): lax.conv_general_dilated(inputs, kernel, (1, 1, 1), ((0, 0), (0, 0), (1,...  61.4 us
    all_gather x1, blocking collectives, local(): lax.all_gather(jnp.einsum('ks,szyx->kzyx', selector.astype(jnp.bfloat16),...  16.3 us
    convert_element_type x4, local copies, waits for them, and re-layouts, convolve(): return jnp.maximum(result, 0.0).astype(jnp.bfloat16)  15.2 us
    all_gather x1, blocking collectives, local(): lax.all_gather(shortened(predicted), 'blocks', axis=0, tiled=True)  13.6 us
    all_gather x1, blocking collectives, local(): everyone = lax.all_gather(tissue_counts, 'blocks', axis=0, tiled=True)  12.7 us
    reduce_sum x1, other arithmetic, unet_level(): pooled = jnp.mean(pooled, axis=(3, 5, 7)).astype(jnp.bfloat16)  9.47 us
    reshape x1, other arithmetic, unet_level(): second_act.astype(jnp.float32)  7.18 us
    ppermute x2, starting transfers between devices, padded(): lax.ppermute(tail, axis, [(i, (i + 1) % count) for i in range(ends)])  6.43 us
  transfers between devices with their start and end apart: 4, of which 0 were waited for; matrix products, arithmetic and copies ran while one was open for 7% of the time, Pallas kernels for 0%

commit v1 on v0

v1 whole, which is shorter than its diff:
```python
import jax
import jax.numpy as jnp
from jax import lax
from jax.experimental import pallas as pl
from jax.experimental.pallas import tpu as pltpu
from jax.sharding import PartitionSpec as P

CORE = 8
MARGIN = 4
MOST = 3
MINC = 4096
F32 = jnp.float32
BF16 = jnp.bfloat16
HBM = pltpu.HBM


def dot(a, b):
    return lax.dot_general(a, b, (((1,), (0,)), ((), ())), preferred_element_type=F32)


def dot_t(a, b):
    return lax.dot_general(a, b, (((1,), (1,)), ((), ())), preferred_element_type=F32)


def iota(shape, dim):
    return lax.broadcasted_iota(jnp.int32, shape, dim)


def tap_rows(flat_ref, rows_ref):
    taps = flat_ref.shape[0]
    for j in range(32):
        block = flat_ref[:, 128 * j : 128 * (j + 1)].astype(F32)
        rows_ref[pl.ds(2 * j, taps, stride=64), :] = block
        rows_ref[pl.ds(2 * j + 1, taps, stride=64), :] = pltpu.roll(block, 64, 1)


def band(w0, w1, w2):
    lower = iota((64, 128), 1) < 64
    d1 = jnp.concatenate([w1, w0], axis=0).T[:64]
    d2 = jnp.concatenate([w2, w1], axis=0).T[:64]
    d0 = jnp.where(lower, pltpu.roll(d1, 64, 1), 0.0)
    d3 = jnp.where(lower, 0.0, pltpu.roll(d2, 64, 1))
    return [d.astype(BF16) for d in (d0, d1, d2, d3)]


def put_bands(out_ref, start, blocks, columns):
    for i, block in enumerate(blocks):
        out_ref[start + 64 * i : start + 64 * (i + 1), columns : columns + 128] = block


def prepare_first(first_hbm, second_hbm, coarse_hbm, head_hbm, raw_hbm, *refs):
    (w1_ref, w2_ref, wh_ref, raw_ref, coarse_ref) = refs[:5]
    (rows_ref, first_ref, second_ref, head_ref, sems) = refs[5:]
    copies = [
        pltpu.make_async_copy(src, dst, sems.at[i])
        for i, (src, dst) in enumerate(
            (
                (second_hbm, second_ref),
                (first_hbm, first_ref),
                (head_hbm, head_ref),
                (raw_hbm, raw_ref),
                (coarse_hbm, coarse_ref),
            )
        )
    ]
    for copy in copies:
        copy.start()

    shape = (256, 27)
    row, lane = iota(shape, 0), iota(shape, 1)
    xo, dz, y = row // 64, (row // 16) % 4, row % 16
    picks = []
    for yy in range(2):
        for xx in range(2):
            dy, dx = y - yy, xo - xx
            valid = (dz < 3) & (dy >= 0) & (dy < 3) & (dx >= 0) & (dx < 3)
            picks.append(jnp.where(valid & (lane == dz * 9 + dy * 3 + dx), 1.0, 0.0).astype(BF16))
    for copy in copies[1:]:
        copy.wait()
    first = jnp.concatenate(
        [first_ref[0, k // 3, k % 3].astype(F32) for k in range(9)], axis=0
    ).astype(BF16)
    base = jnp.concatenate([dot(pick, first) for pick in picks], axis=1)
    for yp in range(7):
        moved = base if yp == 0 else pltpu.roll(base, 2 * yp, 0)
        w1_ref[:, 256 * yp : 256 * (yp + 1)] = moved.astype(BF16)

    wide = (240, 256)
    row, lane = iota(wide, 0), iota(wide, 1)
    yp, xx, y = row // 48, (row // 24) % 2, row % 8
    o = (row // 8) % 3
    head = head_ref[...].astype(F32)
    tiled = jnp.concatenate([head] * 4, axis=1)
    value = jnp.where(o == 0, tiled[0:1], jnp.where(o == 1, tiled[1:2], tiled[2:3]))
    fine = (y // 2 == yp) & (y % 2 == lane // 128) & (xx == (lane // 64) % 2)
    up = (yp == 4) & (y // 2 == lane // 64)
    wh_ref[...] = jnp.where(fine | up, value, 0.0).astype(BF16)

    copies[0].wait()
    tap_rows(second_ref, rows_ref)
    zeros = jnp.zeros((256, 128), BF16)
    for w in range(4):
        for dy in range(3):
            taps = []
            for dx in range(3):
                g0, g1, g2 = (
                    rows_ref[64 * t : 64 * (t + 1), :] for t in range(3 * dy + dx, 27, 9)
                )
                taps.append((g0, 0.5 * (g0 + g1 + g2), 0.5 * (g0 - g1 + g2), g2)[w])
            blocks = band(*taps)
            for yy in range(2):
                put_bands(w2_ref, 256 * (4 * w + dy + yy), blocks, 128 * yy)
        w2_ref[1024 * w : 1024 * w + 256, 128:256] = zeros
        w2_ref[1024 * w + 768 : 1024 * w + 1024, 0:128] = zeros


def prepare_coarse(coarse_ref, wc_ref, rows_ref):
    tap_rows(coarse_ref, rows_ref)
    zeros = jnp.zeros((128, 128), BF16)
    for dz in range(3):
        for dx in range(3):
            blocks = band(
                *(rows_ref[64 * t : 64 * (t + 1), :] for t in range(9 * dz + dx, 9 * dz + 9, 3))
            )
            start = 384 * (3 * dz + dx)
            for half in range(2):
                put_bands(wc_ref, start + 128 * half, blocks, 128 * half)
            wc_ref[start + 256 : start + 384, 0:128] = zeros
            wc_ref[start : start + 128, 128:256] = zeros


def side_by_side(logits):
    lower = iota((24, 128), 1) < 64
    planes = []
    for half in range(2):
        tile = logits[:, 128 * half : 128 * (half + 1)]
        even, odd = tile[:24], tile[24:]
        planes.append(jnp.where(lower, even, pltpu.roll(odd, 64, 1)))
        planes.append(jnp.where(lower, pltpu.roll(even, 64, 1), odd))
    return planes


def tile_kernel(halo_count, tile_count, counts_hbm, offsets_hbm, raw_ref, *refs):
    ysides = refs[: 1 + (halo_count > 2)]
    refs = refs[len(ysides) :]
    (pair_ref, chain_ref, w1_ref, w2_ref, wc_ref, wh_ref, out_ref) = refs[:7]
    (ext_ref, u_ref, a_ref, q_ref, lc_ref, fine_ref, up_ref, pred_ref) = refs[7:15]
    counts_ref, offsets_ref, sems = refs[15:]
    copies = [
        pltpu.make_async_copy(counts_hbm, counts_ref, sems.at[0]),
        pltpu.make_async_copy(offsets_hbm, offsets_ref, sems.at[1]),
    ]
    for copy in copies:
        copy.start()

    halo_index = lax.axis_index("halo")
    gz_index = lax.axis_index("gz")
    tile_index = lax.axis_index("blocks") * 2 + gz_index

    odd_h = halo_index % 2 == 1
    odd_g = gz_index == 1

    def with_rows(own, sides):
        own = own.astype(F32)
        near = sides[0].astype(F32)
        far = sides[1].astype(F32) if len(sides) > 1 else jnp.zeros_like(near)
        below = jnp.where(odd_h, near, far)
        above = jnp.where(odd_h, far, near)
        return jnp.concatenate([below[:, 4:8], own, above[:, 0:4]], axis=1)

    core = with_rows(raw_ref[...], [r[...] for r in ysides])
    pair = with_rows(pair_ref[0], [pair_ref[1 + k] for k in range(len(ysides))])
    chain = with_rows(chain_ref[0], [chain_ref[1 + k] for k in range(len(ysides))])
    edge = jnp.where(odd_g, tile_index == tile_count - 1, tile_index == 0)
    chain = jnp.where(edge, 0.0, chain)
    below = jnp.where(odd_g, pair, chain)
    above = jnp.where(odd_g, chain, pair)
    ext = jnp.concatenate([below, core, above, jnp.zeros((2, 16, 128), F32)], axis=0)
    ext = ext.reshape(26 * 16, 128)
    moved = jnp.where(iota(ext.shape, 1) < 127, pltpu.roll(ext, 127, 1), 0.0)
    ext_ref[0] = ext.astype(BF16).reshape(26, 16, 128)
    ext_ref[1] = moved.astype(BF16).reshape(26, 16, 128)

    row, lane = iota((160, 128), 0), iota((160, 128), 1)
    select = jnp.where(lane == 2 * (row % 80) - 2 + 2 * (row // 80), 1.0, 0.0).astype(BF16)
    for z in range(0, 22, 2):
        around = jnp.concatenate(
            [ext_ref[m, z + d : z + d + 4].reshape(64, 128) for d in range(2) for m in range(2)],
            axis=0,
        )
        u = dot_t(select, around).astype(BF16)
        for d in range(2):
            for m in range(2):
                u_ref[z + d, :, 128 * m : 128 * (m + 1)] = u[
                    80 * m : 80 * (m + 1), 128 * d : 128 * (d + 1)
                ]

    edge_rows, edge_lanes = iota((8, 128), 0), iota((8, 128), 1)
    keep_first = (edge_rows > 0) | (edge_lanes >= 64)
    keep_last = (edge_rows < 1) & (edge_lanes < 64)

    def first_step(k, carry):
        z = 11 * k
        lhs = u_ref[pl.ds(z, 11)].reshape(880, 256)
        for yp in range(7):
            res = jnp.maximum(dot(lhs, w1_ref[:, 256 * yp : 256 * (yp + 1)]), 0.0)
            for d in range(11):
                for yy in range(2):
                    tile = res[80 * d : 80 * d + 72, 128 * yy : 128 * (yy + 1)]
                    head = jnp.where(keep_first, tile[:8], 0.0)
                    tail = jnp.where(keep_last, tile[64:], 0.0)
                    tile = jnp.concatenate([head, tile[8:64], tail], axis=0)
                    a_ref[z + d, yy, yp, :, 0:128] = tile[:64].astype(BF16)
                    after = pltpu.roll(tile, 71, 0)[:64]
                    a_ref[z + d, yy, yp, :, 128:256] = after.astype(BF16)
        return carry

    lax.fori_loop(0, 2, first_step, 0)

    lower_half = iota((64, 128), 1) < 64

    def second_step(k, carry):
        z = 4 * k
        products = []
        for w, (i, j) in enumerate(((0, 2), (1, 2), (2, 1), (1, 3))):
            mixed = []
            for p in range(2):
                first, second = a_ref[z + 2 * p + i], a_ref[z + 2 * p + j]
                mixed.append(first + second if w == 1 else first - second)
            product = None
            for y in range(4):
                lhs = jnp.concatenate(
                    [m[y % 2, y // 2 : y // 2 + 6].reshape(384, 256) for m in mixed], axis=0
                )
                at = 256 * (4 * w + y)
                term = dot(lhs, w2_ref[at : at + 256, :])
                product = term if product is None else product + term
            products.append(product)
        m0, m1, m2, m3 = products
        acts = [m0 + m1 + m2, m1 - m2 - m3]
        acts = [jnp.maximum(act, 0.0).astype(BF16).reshape(2, 6, 64, 256) for act in acts]
        planes = [acts[d % 2][d // 2] for d in range(4)]
        logits = None
        for yp in range(4):
            rows = jnp.concatenate([plane[yp + 1] for plane in planes], axis=0)
            term = dot_t(wh_ref[48 * yp : 48 * (yp + 1), :], rows)
            logits = term if logits is None else logits + term
        for d, plane in enumerate(side_by_side(logits)):
            fine_ref[z + d] = plane
        for d, plane in enumerate(planes):
            full = plane.astype(F32)
            both = full[:, :, :128] + full[:, :, 128:]
            for j in range(3):
                even, odd = both[2 * j], both[2 * j + 1]
                even = even + pltpu.roll(even, 64, 1)
                odd = odd + pltpu.roll(odd, 64, 1)
                q_ref[z + d, j] = jnp.where(lower_half, even, odd)
        return carry

    lax.fori_loop(0, 5, second_step, 0)

    for copy in copies:
        copy.wait()
    slots = counts_ref.shape[2]
    total = jnp.int32(0)
    anchors = [jnp.int32(0)] * MOST
    for s in range(slots):
        dense = counts_ref[0, 0, s] >= MINC
        for j in range(MOST):
            anchors[j] = jnp.where(dense & (total == j), offsets_ref[0, 0, s], anchors[j])
        total = total + dense.astype(jnp.int32)

    rows64 = iota((64, 128), 0)
    for j in range(MOST):
        for k in range(6):
            for m in range(3):
                z = anchors[j] + 2 * k
                mean = (q_ref[z, m] + q_ref[z + 1, m]) * 0.125
                before = jnp.where(rows64 == 0, 0.0, pltpu.roll(mean, 1, 0))
                after = jnp.where(rows64 == 63, 0.0, pltpu.roll(mean, 63, 0))
                for dx, value in enumerate((before, mean, after)):
                    at = 384 * dx + 128 * m
                    lc_ref[j, k, :, at : at + 128] = value.astype(BF16)

    coarse = None
    for dz in range(3):
        lhs = lc_ref[:, dz : dz + 4].reshape(MOST * 256, 1152)
        term = dot(lhs, wc_ref[1152 * dz : 1152 * (dz + 1), :])
        coarse = term if coarse is None else coarse + term
    coarse = jnp.maximum(coarse, 0.0).astype(BF16)
    for j in range(MOST):
        logits = dot_t(wh_ref[192:240, :], coarse[256 * j : 256 * (j + 1)])
        for k, plane in enumerate(side_by_side(logits)):
            up_ref[j, k] = plane

    row, lane = iota((128, 128), 0), iota((128, 128), 1)
    order = jnp.where(lane == 2 * (row % 64) + row // 64, 1.0, 0.0).astype(BF16)
    preds = []
    for j in range(MOST):
        for u in range(CORE):
            logits = fine_ref[anchors[j] + 2 + u] + up_ref[j, u // 2]
            preds.append(jax.nn.sigmoid(logits))
    ordered = dot(jnp.concatenate(preds, axis=0).astype(BF16), order)
    pred_ref[...] = ordered.reshape(MOST, CORE, 3, 8, 128)

    for z in range(16):
        cover = jnp.float32(0.0)
        value = jnp.zeros((3, 8, 128), F32)
        for j in range(MOST):
            u = z - anchors[j]
            uf = u.astype(F32)
            tent = (uf + 1.0) * (CORE - uf) / 20.0
            inside = (j < total) & (u >= 0) & (u < CORE)
            tent = jnp.where(inside, tent, 0.0)
            cover = cover + tent
            value = value + pred_ref[j, jnp.clip(u, 0, CORE - 1)] * tent
        value = value / jnp.maximum(jnp.full((8, 128), cover, F32), 1.0)
        for c in range(3):
            out_ref[c, z] = value[c]


def neighbour_pairs(count, first, closed):
    pairs = []
    for i in range(first, count - 1, 2):
        pairs += [(i, i + 1), (i + 1, i)]
    if closed:
        pairs += [(0, count - 1), (count - 1, 0)]
    return pairs


def local(raw_volume, tissue_counts, patch_core_offsets, w_first, w_second, w_coarse, w_head):
    halo_count = lax.axis_size("halo")
    tile_count = lax.axis_size("blocks") * lax.axis_size("gz")
    vmem = pl.BlockSpec(memory_space=pltpu.VMEM)
    hbm = pl.BlockSpec(memory_space=HBM)

    ysides = [lax.ppermute(raw_volume, "halo", neighbour_pairs(halo_count, 0, False))]
    if halo_count > 2:
        ysides.append(lax.ppermute(raw_volume, "halo", neighbour_pairs(halo_count, 1, False)))

    first_taps = jnp.transpose(w_first, (1, 2, 3, 4, 0))
    w1, w2, wh, raw, coarse = pl.pallas_call(
        prepare_first,
        out_shape=[
            jax.ShapeDtypeStruct((256, 1792), BF16),
            jax.ShapeDtypeStruct((4096, 256), BF16),
            jax.ShapeDtypeStruct((240, 256), BF16),
            jax.ShapeDtypeStruct(raw_volume.shape, BF16),
            jax.ShapeDtypeStruct(w_coarse.shape, BF16),
        ],
        in_specs=[hbm] * 5,
        out_specs=[vmem] * 5,
        scratch_shapes=[
            pltpu.VMEM((27 * 64, 128), F32),
            pltpu.VMEM(first_taps.shape, BF16),
            pltpu.VMEM(w_second.shape, BF16),
            pltpu.VMEM(w_head.shape, BF16),
            pltpu.SemaphoreType.DMA((5,)),
        ],
        compiler_params=pltpu.CompilerParams(vmem_limit_bytes=24 << 20),
        cost_estimate=pl.CostEstimate(flops=1 << 20, bytes_accessed=8 << 20, transcendentals=0),
    )(first_taps, w_second, w_coarse, w_head, raw_volume)

    stack = jnp.stack([raw] + ysides)
    odd = lax.axis_index("gz") == 1
    head, tail = stack[:, :MARGIN], stack[:, -MARGIN:]
    pair = lax.ppermute(jnp.where(odd, head, tail), "gz", [(0, 1), (1, 0)])
    chain = lax.ppermute(
        jnp.where(odd, tail, head), ("blocks", "gz"), neighbour_pairs(tile_count, 1, True)
    )

    wc = pl.pallas_call(
        prepare_coarse,
        out_shape=jax.ShapeDtypeStruct((3456, 256), BF16),
        in_specs=[vmem],
        out_specs=vmem,
        scratch_shapes=[pltpu.VMEM((27 * 64, 128), F32)],
        compiler_params=pltpu.CompilerParams(vmem_limit_bytes=16 << 20),
        cost_estimate=pl.CostEstimate(flops=1 << 20, bytes_accessed=6 << 20, transcendentals=0),
    )(coarse)

    def body(*refs):
        tile_kernel(halo_count, tile_count, *refs)

    return pl.pallas_call(
        body,
        out_shape=jax.ShapeDtypeStruct((3, 16, 8, 128), F32),
        in_specs=[hbm, hbm] + [vmem] * (7 + len(ysides)),
        out_specs=vmem,
        scratch_shapes=[
            pltpu.VMEM((2, 26, 16, 128), BF16),
            pltpu.VMEM((22, 80, 256), BF16),
            pltpu.VMEM((22, 2, 7, 64, 256), BF16),
            pltpu.VMEM((20, 3, 64, 128), F32),
            pltpu.VMEM((MOST, 6, 64, 1152), BF16),
            pltpu.VMEM((20, 24, 128), F32),
            pltpu.VMEM((MOST, 4, 24, 128), F32),
            pltpu.VMEM((MOST, CORE, 3, 8, 128), F32),
            pltpu.SMEM(tissue_counts.shape, jnp.int32),
            pltpu.SMEM(patch_core_offsets.shape, jnp.int32),
            pltpu.SemaphoreType.DMA((2,)),
        ],
        compiler_params=pltpu.CompilerParams(vmem_limit_bytes=40 << 20),
        cost_estimate=pl.CostEstimate(flops=16 << 30, bytes_accessed=5 << 20, transcendentals=0),
    )(tissue_counts, patch_core_offsets, raw, *ysides, pair, chain, w1, w2, wc, wh)


def solution(mesh):
    in_specs = (
        P(("groups", "blocks", "gz"), "halo", None),
        P(("groups", "blocks", "gz"), "halo", None),
        P(("groups", "blocks", "gz"), "halo", None),
        P(),
        P(),
        P(),
        P(),
    )
    out_specs = P(None, ("groups", "blocks", "gz"), "halo", None)
    return jax.shard_map(local, mesh=mesh, in_specs=in_specs, out_specs=out_specs, check_vma=False)
```

time: 174 us -> 32.3 us (0.19)
  matrix products: 62.7 us -> 0 us
  blocking collectives: 42.6 us -> 0 us
  local copies, waits for them, and re-layouts: 32.7 us -> 4.04 us
  other arithmetic: 24.2 us -> 0.02 us
  Pallas kernels: 0 us -> 21 us
  starting transfers between devices: 9 us -> 6.71 us
    conv_general_dilated x3 -> x0, matrix products: 61.4 us -> none  [convolve(): lax.conv_general_dilated(inputs, kernel, (1, 1, 1), ((0, 0), (0, 0), (1,...]
    all_gather x3 -> x0, blocking collectives: 42.6 us -> none  [the longest x1 16.3 us: local(): lax.all_gather(jnp.einsum('ks,szyx->kzyx', selector.astype(jnp.bfloat16),...]
    pallas_call x0 -> x3, Pallas kernels: none -> 21 us  [the longest x1 17.6 us: local(): pl.pallas_call(body, out_shape=jax.ShapeDtypeStruct((3, 16, 8, 128), F32)...]
    convert_element_type x8 -> x0, local copies, waits for them, and re-layouts: 18.4 us -> none  [the longest x4 15.2 us: convolve(): return jnp.maximum(result, 0.0).astype(jnp.bfloat16)]
    reduce_sum x3 -> x0, other arithmetic: 10.2 us -> none  [the longest x1 9.47 us: unet_level(): pooled = jnp.mean(pooled, axis=(3, 5, 7)).astype(jnp.bfloat16)]
    reshape x1 -> x0, other arithmetic: 7.18 us -> none  [unet_level(): second_act.astype(jnp.float32)]
    conv_general_dilated x5 -> x0, local copies, waits for them, and re-layouts: 4.64 us -> none  [convolve(): lax.conv_general_dilated(inputs, kernel, (1, 1, 1), ((0, 0), (0, 0), (1,...]
    reshape x2 -> x0, local copies, waits for them, and re-layouts: 3.61 us -> none  [as_kernel(): flat_weight.reshape(3, 3, 3, channels, channels)]
  transfers between devices with their start and end apart: 4 -> 3, of which waited for: 0 -> 1; matrix products, arithmetic and copies ran while one was open for 7% -> 0% of each run, Pallas kernels for 0% -> 11%
where the time goes in v1:
time: 32.3 us; the launch traced here: 32 us
  Pallas kernels  21 us (65%)
  starting transfers between devices  6.71 us (21%)
  local copies, waits for them, and re-layouts  4.04 us (13%)
    pallas_call x1, Pallas kernels, local(): pl.pallas_call(body, out_shape=jax.ShapeDtypeStruct((3, 16, 8, 128), F32)...  17.6 us
    unnamed x14, local copies, waits for them, and re-layouts  4.04 us
    ppermute x1, starting transfers between devices, local(): lax.ppermute(jnp.where(odd, tail, head), ('blocks', 'gz'), neighbour_pair...  3.7 us
    ppermute x1, starting transfers between devices, local(): lax.ppermute(raw_volume, 'halo', neighbour_pairs(halo_count, 0, False))  2.94 us
    pallas_call x1, Pallas kernels, local(): pl.pallas_call(prepare_first, out_shape=[jax.ShapeDtypeStruct((256, 1792)...  2.2 us
    pallas_call x1, Pallas kernels, local(): pl.pallas_call(prepare_coarse, out_shape=jax.ShapeDtypeStruct((3456, 256)...  1.21 us
  transfers between devices with their start and end apart: 3, of which 1 were waited for; matrix products, arithmetic and copies ran while one was open for 0% of the time, Pallas kernels for 11%

profile of v1, /device:TPU:0, one launch (start us, length us, event | category | flops | bytes accessed | tf_op | source)
XLA Modules:
  0.0 32.0 jit_solution(12709571363789084381)
XLA Ops:
  0.0 0.0 copy-start.6
  0.0 0.0 copy-start.5
  0.0 2.9 %collective-permute-start = (bf16[16,8,128]{2,1,0:T(8,128)(2,1)}, bf16[16,8,128]{2,1,0:T(8,128)(2,1)S(1)}, u32[]{:S(2)}, u32[]{:S(2)}) collective-permute-start(bf16[16,8,128]{2,1,0:T(8,128)(2,1)} %raw_hbm.1), channel_id=1, source_target_pairs={{0,2},{2,0},{1,3},{3,1},{4,6},{6,4},{5,7},{7,5},{8,10},{10,8},{9,1... | collective-permute-start | bytes 98312 | tf_op jit(solution)/shard_map/ppermute | solution.py:337
  2.9 0.0 copy-start
  2.9 0.9 %copy-done = bf16[27,4096]{1,0:T(8,128)(2,1)S(1)} copy-done((bf16[27,4096]{1,0:T(8,128)(2,1)S(1)}, bf16[27,4096]{1,0:T(8,128)(2,1)}, u32[]{:S(2)}) %copy-start) | copy-done | bytes 221208
  3.9 0.0 copy-start.1
  3.9 0.9 %copy-done.1 = bf16[27,4096]{1,0:T(8,128)(2,1)S(1)} copy-done((bf16[27,4096]{1,0:T(8,128)(2,1)S(1)}, bf16[27,4096]{1,0:T(8,128)(2,1)}, u32[]{:S(2)}) %copy-start.1) | copy-done | bytes 221208
  4.8 0.0 copy-start.2
  4.8 0.8 %copy-done.2 = bf16[16,8,128]{2,1,0:T(8,128)(2,1)S(1)} copy-done((bf16[16,8,128]{2,1,0:T(8,128)(2,1)S(1)}, bf16[16,8,128]{2,1,0:T(8,128)(2,1)}, u32[]{:S(2)}) %copy-start.2) | copy-done | bytes 32792
  5.6 0.0 copy-start.3
  5.6 0.7 %copy-done.3 = bf16[64,1,3,3,3]{0,4,3,2,1:T(4,128)(2,1)S(1)} copy-done((bf16[64,1,3,3,3]{0,4,3,2,1:T(4,128)(2,1)S(1)}, bf16[64,1,3,3,3]{0,4,3,2,1:T(4,128)(2,1)}, u32[]{:S(2)}) %copy-start.3) | copy-done | bytes 3480
  6.3 0.0 copy-start.4
  6.3 0.7 %copy-done.4 = bf16[3,64]{1,0:T(4,128)(2,1)S(1)} copy-done((bf16[3,64]{1,0:T(4,128)(2,1)S(1)}, bf16[3,64]{1,0:T(4,128)(2,1)}, u32[]{:S(2)}) %copy-start.4) | copy-done | bytes 408
  7.0 2.2 %shard_map.73 = (bf16[256,1792]{1,0:T(8,128)(2,1)S(1)}, bf16[4096,256]{1,0:T(8,128)(2,1)S(1)}, bf16[240,256]{1,0:T(8,128)(2,1)S(1)}, bf16[16,8,128]{2,1,0:T(8,128)(2,1)S(1)}, bf16[27,4096]{1,0:T(8,128)(2,1)S(1)}) custom-call(bf16[1,3,3,3,64]{4,3,2,1,0:T(4,128)(2,1)S(1)} %bitcast.5, bf16[27,4096]{1,0:T(8,128)(2,1)S(1)} %copy-done, ...), custom_call_target="tpu_custom_call" | custom-call | flops 1048576 | bytes 8388608 | tf_op jit(solution)/shard_map/pallas_call | solution.py:342
  9.2 0.0 collective-permute-done.refs_3_
  9.2 0.1 collective-permute-start.1
  9.3 3.7 %collective-permute-start.2 = (bf16[2,4,8,128]{3,2,1,0:T(8,128)(2,1)S(1)}, bf16[2,4,8,128]{3,2,1,0:T(8,128)(2,1)S(1)}, u32[]{:S(2)}, u32[]{:S(2)}) collective-permute-start(bf16[2,4,8,128]{3,2,1,0:T(8,128)(2,1)S(1)} %get-tuple-element.15), channel_id=1, source_target_pairs={{1,4},{4,1},{5,8},{8,5},{9,12},{12,9},{0,13},{13,0},{3,6},{6,3},{7... | collective-permute-start | bytes 49160 | tf_op jit(solution)/shard_map/ppermute | solution.py:368
  13.0 1.2 %shard_map.74.refs_8_ = bf16[3456,256]{1,0:T(8,128)(2,1)S(1)} custom-call(bf16[27,4096]{1,0:T(8,128)(2,1)S(1)} %get-tuple-element.13.coarse_ref), custom_call_target="tpu_custom_call" | custom-call | flops 1048576 | bytes 6291456 | tf_op jit(solution)/shard_map/pallas_call | solution.py:372
  14.2 0.0 collective-permute-done.1.refs_4_
  14.2 0.2 collective-permute-done.2.refs_5_
  14.5 0.0 copy-done.6
  14.5 0.0 copy-done.5
  14.5 17.6 %shard_map.75 = f32[3,16,8,128]{3,2,1,0:T(8,128)} custom-call(s32[1,1,4]{2,1,0:T(1,128)S(1)} %copy-done.5, s32[1,1,4]{2,1,0:T(1,128)S(1)} %copy-done.6, bf16[16,8,128]{2,1,0:T(8,128)(2,1)S(1)} %get-tuple-element.10.refs_2_, bf16[16,8,128]{2,1,0:T(8,128)(2,1)S(1)} %collective-permute-done.refs_3_, bf16[2,4,8,128]{3,2,1,0:T(8,128)(2,1)S(1)} %collective-permute-done.1.refs_4_, ...), custom_call_target="tpu_custom_call" | custom-call | flops 17179869184 | bytes 5242880 | tf_op jit(solution)/shard_map/pallas_call | solution.py:385
  (2 shorter events, 0.0 us)
Async XLA Ops:
  0.0 14.5 %copy-start.6 = (s32[1,1,4]{2,1,0:T(1,128)S(1)}, s32[1,1,4]{2,1,0:T(1,128)}, u32[]{:S(2)}) copy-start(s32[1,1,4]{2,1,0:T(1,128)} %refs_1_.1) | copy-start | bytes 52
  0.0 14.5 %copy-start.5 = (s32[1,1,4]{2,1,0:T(1,128)S(1)}, s32[1,1,4]{2,1,0:T(1,128)}, u32[]{:S(2)}) copy-start(s32[1,1,4]{2,1,0:T(1,128)} %refs_0_.1) | copy-start | bytes 52
  0.0 9.2 %collective-permute-start = (bf16[16,8,128]{2,1,0:T(8,128)(2,1)}, bf16[16,8,128]{2,1,0:T(8,128)(2,1)S(1)}, u32[]{:S(2)}, u32[]{:S(2)}) collective-permute-start(bf16[16,8,128]{2,1,0:T(8,128)(2,1)} %raw_hbm.1), channel_id=1, source_target_pairs={{0,2},{2,0},{1,3},{3,1},{4,6},{6,4},{5,7},{7,5},{8,10},{10,8},{9,1... | collective-permute-start | bytes 98312 | tf_op jit(solution)/shard_map/ppermute | solution.py:337
  2.9 0.9 %copy-start = (bf16[27,4096]{1,0:T(8,128)(2,1)S(1)}, bf16[27,4096]{1,0:T(8,128)(2,1)}, u32[]{:S(2)}) copy-start(bf16[27,4096]{1,0:T(8,128)(2,1)} %second_hbm.1) | copy-start | bytes 663556
  3.9 0.9 %copy-start.1 = (bf16[27,4096]{1,0:T(8,128)(2,1)S(1)}, bf16[27,4096]{1,0:T(8,128)(2,1)}, u32[]{:S(2)}) copy-start(bf16[27,4096]{1,0:T(8,128)(2,1)} %coarse_hbm.1) | copy-start | bytes 663556
  4.8 0.8 %copy-start.2 = (bf16[16,8,128]{2,1,0:T(8,128)(2,1)S(1)}, bf16[16,8,128]{2,1,0:T(8,128)(2,1)}, u32[]{:S(2)}) copy-start(bf16[16,8,128]{2,1,0:T(8,128)(2,1)} %raw_hbm.1) | copy-start | bytes 98308
  5.6 0.7 %copy-start.3 = (bf16[64,1,3,3,3]{0,4,3,2,1:T(4,128)(2,1)S(1)}, bf16[64,1,3,3,3]{0,4,3,2,1:T(4,128)(2,1)}, u32[]{:S(2)}) copy-start(bf16[64,1,3,3,3]{0,4,3,2,1:T(4,128)(2,1)} %param.10) | copy-start | bytes 10372
  6.3 0.7 %copy-start.4 = (bf16[3,64]{1,0:T(4,128)(2,1)S(1)}, bf16[3,64]{1,0:T(4,128)(2,1)}, u32[]{:S(2)}) copy-start(bf16[3,64]{1,0:T(4,128)(2,1)} %head_hbm.1) | copy-start | bytes 1156
  9.2 5.0 %collective-permute-start.1 = (bf16[2,4,8,128]{3,2,1,0:T(8,128)(2,1)S(1)}, bf16[2,4,8,128]{3,2,1,0:T(8,128)(2,1)S(1)}, u32[]{:S(2)}, u32[]{:S(2)}) collective-permute-start(bf16[2,4,8,128]{3,2,1,0:T(8,128)(2,1)S(1)} %broadcast_select_fusion.1), channel_id=1, source_target_pairs={{0,1},{1,0},{2,3},{3,2},{4,5},{5,4},{6,7},{7,6},{8,9},{9,8},{10,11... | collective-permute-start | bytes 49160 | tf_op jit(solution)/shard_map/ppermute | solution.py:367
  9.3 5.1 %collective-permute-start.2 = (bf16[2,4,8,128]{3,2,1,0:T(8,128)(2,1)S(1)}, bf16[2,4,8,128]{3,2,1,0:T(8,128)(2,1)S(1)}, u32[]{:S(2)}, u32[]{:S(2)}) collective-permute-start(bf16[2,4,8,128]{3,2,1,0:T(8,128)(2,1)S(1)} %get-tuple-element.15), channel_id=1, source_target_pairs={{1,4},{4,1},{5,8},{8,5},{9,12},{12,9},{0,13},{13,0},{3,6},{6,3},{7... | collective-permute-start | bytes 49160 | tf_op jit(solution)/shard_map/ppermute | solution.py:368

commit v2 on v1

--- a/solution.py
+++ b/solution.py
@@ -48,17 +48,16 @@
         out_ref[start + 64 * i : start + 64 * (i + 1), columns : columns + 128] = block
 
 
-def prepare_first(first_hbm, second_hbm, coarse_hbm, head_hbm, raw_hbm, *refs):
-    (w1_ref, w2_ref, wh_ref, raw_ref, coarse_ref) = refs[:5]
-    (rows_ref, first_ref, second_ref, head_ref, sems) = refs[5:]
+def prepare_second(first_hbm, second_hbm, coarse_hbm, head_hbm, raw_hbm, *refs):
+    (w2_ref, first_ref, coarse_ref, head_ref, raw_ref, rows_ref, second_ref, sems) = refs
     copies = [
         pltpu.make_async_copy(src, dst, sems.at[i])
         for i, (src, dst) in enumerate(
             (
                 (second_hbm, second_ref),
+                (raw_hbm, raw_ref),
                 (first_hbm, first_ref),
                 (head_hbm, head_ref),
-                (raw_hbm, raw_ref),
                 (coarse_hbm, coarse_ref),
             )
         )
@@ -66,39 +65,12 @@
     for copy in copies:
         copy.start()
 
-    shape = (256, 27)
-    row, lane = iota(shape, 0), iota(shape, 1)
-    xo, dz, y = row // 64, (row // 16) % 4, row % 16
-    picks = []
-    for yy in range(2):
-        for xx in range(2):
-            dy, dx = y - yy, xo - xx
-            valid = (dz < 3) & (dy >= 0) & (dy < 3) & (dx >= 0) & (dx < 3)
-            picks.append(jnp.where(valid & (lane == dz * 9 + dy * 3 + dx), 1.0, 0.0).astype(BF16))
-    for copy in copies[1:]:
-        copy.wait()
-    first = jnp.concatenate(
-        [first_ref[0, k // 3, k % 3].astype(F32) for k in range(9)], axis=0
-    ).astype(BF16)
-    base = jnp.concatenate([dot(pick, first) for pick in picks], axis=1)
-    for yp in range(7):
-        moved = base if yp == 0 else pltpu.roll(base, 2 * yp, 0)
-        w1_ref[:, 256 * yp : 256 * (yp + 1)] = moved.astype(BF16)
-
-    wide = (240, 256)
-    row, lane = iota(wide, 0), iota(wide, 1)
-    yp, xx, y = row // 48, (row // 24) % 2, row % 8
-    o = (row // 8) % 3
-    head = head_ref[...].astype(F32)
-    tiled = jnp.concatenate([head] * 4, axis=1)
-    value = jnp.where(o == 0, tiled[0:1], jnp.where(o == 1, tiled[1:2], tiled[2:3]))
-    fine = (y // 2 == yp) & (y % 2 == lane // 128) & (xx == (lane // 64) % 2)
-    up = (yp == 4) & (y // 2 == lane // 64)
-    wh_ref[...] = jnp.where(fine | up, value, 0.0).astype(BF16)
-
+    zeros = jnp.zeros((256, 128), BF16)
+    for w in range(4):
+        w2_ref[1024 * w : 1024 * w + 256, 128:256] = zeros
+        w2_ref[1024 * w + 768 : 1024 * w + 1024, 0:128] = zeros
     copies[0].wait()
     tap_rows(second_ref, rows_ref)
-    zeros = jnp.zeros((256, 128), BF16)
     for w in range(4):
         for dy in range(3):
             taps = []
@@ -110,11 +82,40 @@
             blocks = band(*taps)
             for yy in range(2):
                 put_bands(w2_ref, 256 * (4 * w + dy + yy), blocks, 128 * yy)
-        w2_ref[1024 * w : 1024 * w + 256, 128:256] = zeros
-        w2_ref[1024 * w + 768 : 1024 * w + 1024, 0:128] = zeros
-
-
-def prepare_coarse(coarse_ref, wc_ref, rows_ref):
+    for copy in copies[1:]:
+        copy.wait()
+
+
+def prepare_rest(first_ref, coarse_ref, head_ref, w1_ref, wc_ref, wh_ref, rows_ref):
+    shape = (256, 27)
+    row, lane = iota(shape, 0), iota(shape, 1)
+    xo, dz, y = row // 64, (row // 16) % 4, row % 16
+    first = jnp.concatenate(
+        [first_ref[0, k // 3, k % 3].astype(F32) for k in range(9)], axis=0
+    ).astype(BF16)
+    parts = []
+    for yy in range(2):
+        for xx in range(2):
+            dy, dx = y - yy, xo - xx
+            valid = (dz < 3) & (dy >= 0) & (dy < 3) & (dx >= 0) & (dx < 3)
+            pick = jnp.where(valid & (lane == dz * 9 + dy * 3 + dx), 1.0, 0.0).astype(BF16)
+            parts.append(dot(pick, first))
+    base = jnp.concatenate(parts, axis=1)
+    for yp in range(7):
+        moved = base if yp == 0 else pltpu.roll(base, 2 * yp, 0)
+        w1_ref[:, 256 * yp : 256 * (yp + 1)] = moved.astype(BF16)
+
+    wide = (240, 256)
+    row, lane = iota(wide, 0), iota(wide, 1)
+    yp, xx, y = row // 48, (row // 24) % 2, row % 8
+    o = (row // 8) % 3
+    head = head_ref[...].astype(F32)
+    tiled = jnp.concatenate([head] * 4, axis=1)
+    value = jnp.where(o == 0, tiled[0:1], jnp.where(o == 1, tiled[1:2], tiled[2:3]))
+    fine = (y // 2 == yp) & (y % 2 == lane // 128) & (xx == (lane // 64) % 2)
+    up = (yp == 4) & (y // 2 == lane // 64)
+    wh_ref[...] = jnp.where(fine | up, value, 0.0).astype(BF16)
+
     tap_rows(coarse_ref, rows_ref)
     zeros = jnp.zeros((128, 128), BF16)
     for dz in range(3):
@@ -144,8 +145,8 @@
     ysides = refs[: 1 + (halo_count > 2)]
     refs = refs[len(ysides) :]
     (pair_ref, chain_ref, w1_ref, w2_ref, wc_ref, wh_ref, out_ref) = refs[:7]
-    (ext_ref, u_ref, a_ref, q_ref, lc_ref, fine_ref, up_ref, pred_ref) = refs[7:15]
-    counts_ref, offsets_ref, sems = refs[15:]
+    (ext_ref, u_ref, a_ref, s_ref, q_ref, lc_ref, fine_ref, up_ref, pred_ref) = refs[7:16]
+    counts_ref, offsets_ref, sems = refs[16:]
     copies = [
         pltpu.make_async_copy(counts_hbm, counts_ref, sems.at[0]),
         pltpu.make_async_copy(offsets_hbm, offsets_ref, sems.at[1]),
@@ -240,13 +241,8 @@
         acts = [m0 + m1 + m2, m1 - m2 - m3]
         acts = [jnp.maximum(act, 0.0).astype(BF16).reshape(2, 6, 64, 256) for act in acts]
         planes = [acts[d % 2][d // 2] for d in range(4)]
-        logits = None
-        for yp in range(4):
-            rows = jnp.concatenate([plane[yp + 1] for plane in planes], axis=0)
-            term = dot_t(wh_ref[48 * yp : 48 * (yp + 1), :], rows)
-            logits = term if logits is None else logits + term
-        for d, plane in enumerate(side_by_side(logits)):
-            fine_ref[z + d] = plane
+        for d, plane in enumerate(planes):
+            s_ref[z + d] = plane[1:5]
         for d, plane in enumerate(planes):
             full = plane.astype(F32)
             both = full[:, :, :128] + full[:, :, 128:]
@@ -258,6 +254,14 @@
         return carry
 
     lax.fori_loop(0, 5, second_step, 0)
+
+    for z in range(2, 18, 4):
+        logits = None
+        for yp in range(4):
+            term = dot_t(wh_ref[48 * yp : 48 * (yp + 1), :], s_ref[z : z + 4, yp].reshape(256, 256))
+            logits = term if logits is None else logits + term
+        for d, plane in enumerate(side_by_side(logits)):
+            fine_ref[z - 2 + d] = plane
 
     for copy in copies:
         copy.wait()
@@ -298,7 +302,7 @@
     preds = []
     for j in range(MOST):
         for u in range(CORE):
-            logits = fine_ref[anchors[j] + 2 + u] + up_ref[j, u // 2]
+            logits = fine_ref[anchors[j] + u] + up_ref[j, u // 2]
             preds.append(jax.nn.sigmoid(logits))
     ordered = dot(jnp.concatenate(preds, axis=0).astype(BF16), order)
     pred_ref[...] = ordered.reshape(MOST, CORE, 3, 8, 128)
@@ -319,12 +323,21 @@
             out_ref[c, z] = value[c]
 
 
-def neighbour_pairs(count, first, closed):
+def neighbour_pairs(count, first):
     pairs = []
     for i in range(first, count - 1, 2):
         pairs += [(i, i + 1), (i + 1, i)]
-    if closed:
-        pairs += [(0, count - 1), (count - 1, 0)]
+    return pairs
+
+
+def chain_pairs(tile_count, halo_count):
+    def device(tile, h):
+        return (tile // 2 * halo_count + h) * 2 + tile % 2
+
+    pairs = []
+    for h in range(halo_count):
+        pairs += [(device(a, h), device(b, h)) for a, b in neighbour_pairs(tile_count, 1)]
+        pairs += [(device(end, h), device(end, h ^ 1)) for end in (0, tile_count - 1)]
     return pairs
 
 
@@ -334,50 +347,51 @@
     vmem = pl.BlockSpec(memory_space=pltpu.VMEM)
     hbm = pl.BlockSpec(memory_space=HBM)
 
-    ysides = [lax.ppermute(raw_volume, "halo", neighbour_pairs(halo_count, 0, False))]
+    ysides = [lax.ppermute(raw_volume, "halo", neighbour_pairs(halo_count, 0))]
     if halo_count > 2:
-        ysides.append(lax.ppermute(raw_volume, "halo", neighbour_pairs(halo_count, 1, False)))
+        ysides.append(lax.ppermute(raw_volume, "halo", neighbour_pairs(halo_count, 1)))
 
     first_taps = jnp.transpose(w_first, (1, 2, 3, 4, 0))
-    w1, w2, wh, raw, coarse = pl.pallas_call(
-        prepare_first,
-        out_shape=[
-            jax.ShapeDtypeStruct((256, 1792), BF16),
-            jax.ShapeDtypeStruct((4096, 256), BF16),
-            jax.ShapeDtypeStruct((240, 256), BF16),
-            jax.ShapeDtypeStruct(raw_volume.shape, BF16),
-            jax.ShapeDtypeStruct(w_coarse.shape, BF16),
-        ],
+    held = [first_taps, w_coarse, w_head, raw_volume]
+    sources = [first_taps, w_second, w_coarse, w_head, raw_volume]
+    w2, first, coarse, head, raw = pl.pallas_call(
+        prepare_second,
+        out_shape=[jax.ShapeDtypeStruct((4096, 256), BF16)]
+        + [jax.ShapeDtypeStruct(x.shape, BF16) for x in held],
         in_specs=[hbm] * 5,
         out_specs=[vmem] * 5,
         scratch_shapes=[
             pltpu.VMEM((27 * 64, 128), F32),
-            pltpu.VMEM(first_taps.shape, BF16),
             pltpu.VMEM(w_second.shape, BF16),
-            pltpu.VMEM(w_head.shape, BF16),
             pltpu.SemaphoreType.DMA((5,)),
         ],
         compiler_params=pltpu.CompilerParams(vmem_limit_bytes=24 << 20),
         cost_estimate=pl.CostEstimate(flops=1 << 20, bytes_accessed=8 << 20, transcendentals=0),
-    )(first_taps, w_second, w_coarse, w_head, raw_volume)
+    )(*(pltpu.with_memory_space_constraint(x, HBM) for x in sources))
 
     stack = jnp.stack([raw] + ysides)
     odd = lax.axis_index("gz") == 1
-    head, tail = stack[:, :MARGIN], stack[:, -MARGIN:]
-    pair = lax.ppermute(jnp.where(odd, head, tail), "gz", [(0, 1), (1, 0)])
+    first_layers, last_layers = stack[:, :MARGIN], stack[:, -MARGIN:]
+    pair = lax.ppermute(jnp.where(odd, first_layers, last_layers), "gz", [(0, 1), (1, 0)])
     chain = lax.ppermute(
-        jnp.where(odd, tail, head), ("blocks", "gz"), neighbour_pairs(tile_count, 1, True)
+        jnp.where(odd, last_layers, first_layers),
+        ("blocks", "halo", "gz"),
+        chain_pairs(tile_count, halo_count),
     )
 
-    wc = pl.pallas_call(
-        prepare_coarse,
-        out_shape=jax.ShapeDtypeStruct((3456, 256), BF16),
-        in_specs=[vmem],
-        out_specs=vmem,
+    w1, wc, wh = pl.pallas_call(
+        prepare_rest,
+        out_shape=[
+            jax.ShapeDtypeStruct((256, 1792), BF16),
+            jax.ShapeDtypeStruct((3456, 256), BF16),
+            jax.ShapeDtypeStruct((240, 256), BF16),
+        ],
+        in_specs=[vmem] * 3,
+        out_specs=[vmem] * 3,
         scratch_shapes=[pltpu.VMEM((27 * 64, 128), F32)],
         compiler_params=pltpu.CompilerParams(vmem_limit_bytes=16 << 20),
         cost_estimate=pl.CostEstimate(flops=1 << 20, bytes_accessed=6 << 20, transcendentals=0),
-    )(coarse)
+    )(first, coarse, head)
 
     def body(*refs):
         tile_kernel(halo_count, tile_count, *refs)
@@ -391,9 +405,10 @@
             pltpu.VMEM((2, 26, 16, 128), BF16),
             pltpu.VMEM((22, 80, 256), BF16),
             pltpu.VMEM((22, 2, 7, 64, 256), BF16),
+            pltpu.VMEM((20, 4, 64, 256), BF16),
             pltpu.VMEM((20, 3, 64, 128), F32),
             pltpu.VMEM((MOST, 6, 64, 1152), BF16),
-            pltpu.VMEM((20, 24, 128), F32),
+            pltpu.VMEM((16, 24, 128), F32),
             pltpu.VMEM((MOST, 4, 24, 128), F32),
             pltpu.VMEM((MOST, CORE, 3, 8, 128), F32),
             pltpu.SMEM(tissue_counts.shape, jnp.int32),
@@ -402,7 +417,18 @@
         ],
         compiler_params=pltpu.CompilerParams(vmem_limit_bytes=40 << 20),
         cost_estimate=pl.CostEstimate(flops=16 << 30, bytes_accessed=5 << 20, transcendentals=0),
-    )(tissue_counts, patch_core_offsets, raw, *ysides, pair, chain, w1, w2, wc, wh)
+    )(
+        pltpu.with_memory_space_constraint(tissue_counts, HBM),
+        pltpu.with_memory_space_constraint(patch_core_offsets, HBM),
+        raw,
+        *ysides,
+        pair,
+        chain,
+        w1,
+        w2,
+        wc,
+        wh,
+    )
 
 
 def solution(mesh):

time: 32.3 us -> 26.1 us (0.81)
  local copies, waits for them, and re-layouts: 4.04 us -> 0 us
  starting transfers between devices: 6.71 us -> 4.88 us
    unnamed x14 -> x0, local copies, waits for them, and re-layouts: 4.04 us -> none
    ppermute x3, starting transfers between devices: 6.71 us -> 4.88 us  [the longest x1 2.94 us: local(): ysides = [lax.ppermute(raw_volume, 'halo', neighbour_pairs(halo_count, 0))]]
    pallas_call x1, Pallas kernels: 17.6 us -> 16.7 us  [local(): pl.pallas_call(body, out_shape=jax.ShapeDtypeStruct((3, 16, 8, 128), F32)...]
    pallas_call x2, Pallas kernels: 3.41 us -> 3.91 us  [the longest x1 2.29 us: local(): pl.pallas_call(prepare_second, out_shape=[jax.ShapeDtypeStruct((4096, 256...]
  transfers between devices with their start and end apart: 3 -> 3, of which waited for: 1 -> 1; matrix products, arithmetic and copies ran while one was open for 0% -> 0% of each run, Pallas kernels for 11% -> 15%
where the time goes in v2:
time: 26.1 us; the launch traced here: 25.9 us
  Pallas kernels  20.7 us (79%)
  starting transfers between devices  4.88 us (19%)
  waiting for transfers between devices  0.3 us (1%)
    pallas_call x1, Pallas kernels, local(): pl.pallas_call(body, out_shape=jax.ShapeDtypeStruct((3, 16, 8, 128), F32)...  16.7 us
    ppermute x1, starting transfers between devices, local(): ysides = [lax.ppermute(raw_volume, 'halo', neighbour_pairs(halo_count, 0))]  2.94 us
    pallas_call x1, Pallas kernels, local(): pl.pallas_call(prepare_second, out_shape=[jax.ShapeDtypeStruct((4096, 256...  2.29 us
    ppermute x1, starting transfers between devices, local(): lax.ppermute(jnp.where(odd, last_layers, first_layers), ('blocks', 'halo'...  1.87 us
    pallas_call x1, Pallas kernels, local(): pl.pallas_call(prepare_rest, out_shape=[jax.ShapeDtypeStruct((256, 1792),...  1.62 us
  transfers between devices with their start and end apart: 3, of which 1 were waited for; matrix products, arithmetic and copies ran while one was open for 0% of the time, Pallas kernels for 15%

profile of v2, /device:TPU:0, one launch (start us, length us, event | category | flops | bytes accessed | tf_op | source)
XLA Modules:
  0.0 25.9 jit_solution(14133201740178981265)
XLA Ops:
  0.0 2.9 %collective-permute-start = (bf16[16,8,128]{2,1,0:T(8,128)(2,1)}, bf16[16,8,128]{2,1,0:T(8,128)(2,1)S(1)}, u32[]{:S(2)}, u32[]{:S(2)}) collective-permute-start(bf16[16,8,128]{2,1,0:T(8,128)(2,1)} %raw_hbm.1), channel_id=1, source_target_pairs={{0,2},{2,0},{1,3},{3,1},{4,6},{6,4},{5,7},{7,5},{8,10},{10,8},{9,1... | collective-permute-start | bytes 98312 | tf_op jit(solution)/shard_map/ppermute | solution.py:350
  2.9 2.3 %shard_map.73 = (bf16[4096,256]{1,0:T(8,128)(2,1)S(1)}, bf16[1,3,3,3,64]{4,3,2,1,0:T(4,128)(2,1)S(1)}, bf16[27,4096]{1,0:T(8,128)(2,1)S(1)}, bf16[3,64]{1,0:T(4,128)(2,1)S(1)}, bf16[16,8,128]{2,1,0:T(8,128)(2,1)S(1)}) custom-call(bf16[1,3,3,3,64]{4,3,2,1,0:T(4,128)(2,1)} %bitcast.5, bf16[27,4096]{1,0:T(8,128)(2,1)} %second_hbm.1, ...), custom_call_target="tpu_custom_call" | custom-call | flops 1048576 | bytes 8388608 | tf_op jit(solution)/shard_map/pallas_call | solution.py:357
  5.2 0.0 collective-permute-done.refs_3_
  5.3 0.1 collective-permute-start.1
  5.4 1.9 %collective-permute-start.2 = (bf16[2,4,8,128]{3,2,1,0:T(8,128)(2,1)S(1)}, bf16[2,4,8,128]{3,2,1,0:T(8,128)(2,1)S(1)}, u32[]{:S(2)}, u32[]{:S(2)}) collective-permute-start(bf16[2,4,8,128]{3,2,1,0:T(8,128)(2,1)S(1)} %get-tuple-element.21), channel_id=1, source_target_pairs={{1,4},{4,1},{5,8},{8,5},{9,12},{12,9},{0,2},{13,15},{3,6},{6,3},{7... | collective-permute-start | bytes 49160 | tf_op jit(solution)/shard_map/ppermute | solution.py:376
  7.2 1.6 %shard_map.74 = (bf16[256,1792]{1,0:T(8,128)(2,1)S(1)}, bf16[3456,256]{1,0:T(8,128)(2,1)S(1)}, bf16[240,256]{1,0:T(8,128)(2,1)S(1)}) custom-call(bf16[1,3,3,3,64]{4,3,2,1,0:T(4,128)(2,1)S(1)} %get-tuple-element.14.first_ref, bf16[27,4096]{1,0:T(8,128)(2,1)S(1)} %get-tuple-element.15.coarse_ref, bf16[3,64]{1,0:T(4,128)(2,1)S(1)} %get-tuple-element.16.head_ref), custom_call_target="tpu_custom_call" | custom-call | flops 1048576 | bytes 6291456 | tf_op jit(solution)/shard_map/pallas_call | solution.py:382
  8.9 0.0 collective-permute-done.1.refs_4_
  8.9 0.3 %collective-permute-done.2.refs_5_ = bf16[2,4,8,128]{3,2,1,0:T(8,128)(2,1)S(1)} collective-permute-done((bf16[2,4,8,128]{3,2,1,0:T(8,128)(2,1)S(1)}, bf16[2,4,8,128]{3,2,1,0:T(8,128)(2,1)S(1)}, u32[]{:S(2)}, u32[]{:S(2)}) %collective-permute-start.2) | collective-permute-done | bytes 16416 | tf_op jit(solution)/shard_map/ppermute | solution.py:376
  9.2 16.7 %shard_map.75 = f32[3,16,8,128]{3,2,1,0:T(8,128)} custom-call(s32[1,1,4]{2,1,0:T(1,128)} %refs_0_.1, s32[1,1,4]{2,1,0:T(1,128)} %refs_1_.1, bf16[16,8,128]{2,1,0:T(8,128)(2,1)S(1)} %get-tuple-element.13.refs_2_, bf16[16,8,128]{2,1,0:T(8,128)(2,1)S(1)} %collective-permute-done.refs_3_, bf16[2,4,8,128]{3,2,1,0:T(8,128)(2,1)S(1)} %collective-permute-done.1.refs_4_, ...), custom_call_target="tpu_custom_call" | custom-call | flops 17179869184 | bytes 5242880 | tf_op jit(solution)/shard_map/pallas_call | solution.py:399
  (2 shorter events, 0.0 us)
Async XLA Ops:
  0.0 5.2 %collective-permute-start = (bf16[16,8,128]{2,1,0:T(8,128)(2,1)}, bf16[16,8,128]{2,1,0:T(8,128)(2,1)S(1)}, u32[]{:S(2)}, u32[]{:S(2)}) collective-permute-start(bf16[16,8,128]{2,1,0:T(8,128)(2,1)} %raw_hbm.1), channel_id=1, source_target_pairs={{0,2},{2,0},{1,3},{3,1},{4,6},{6,4},{5,7},{7,5},{8,10},{10,8},{9,1... | collective-permute-start | bytes 98312 | tf_op jit(solution)/shard_map/ppermute | solution.py:350
  5.3 3.6 %collective-permute-start.1 = (bf16[2,4,8,128]{3,2,1,0:T(8,128)(2,1)S(1)}, bf16[2,4,8,128]{3,2,1,0:T(8,128)(2,1)S(1)}, u32[]{:S(2)}, u32[]{:S(2)}) collective-permute-start(bf16[2,4,8,128]{3,2,1,0:T(8,128)(2,1)S(1)} %broadcast_select_fusion.1), channel_id=1, source_target_pairs={{0,1},{1,0},{2,3},{3,2},{4,5},{5,4},{6,7},{7,6},{8,9},{9,8},{10,11... | collective-permute-start | bytes 49160 | tf_op jit(solution)/shard_map/ppermute | solution.py:375
  5.4 3.8 %collective-permute-start.2 = (bf16[2,4,8,128]{3,2,1,0:T(8,128)(2,1)S(1)}, bf16[2,4,8,128]{3,2,1,0:T(8,128)(2,1)S(1)}, u32[]{:S(2)}, u32[]{:S(2)}) collective-permute-start(bf16[2,4,8,128]{3,2,1,0:T(8,128)(2,1)S(1)} %get-tuple-element.21), channel_id=1, source_target_pairs={{1,4},{4,1},{5,8},{8,5},{9,12},{12,9},{0,2},{13,15},{3,6},{6,3},{7... | collective-permute-start | bytes 49160 | tf_op jit(solution)/shard_map/ppermute | solution.py:376

commit v3 on v2

--- a/solution.py
+++ b/solution.py
@@ -220,40 +220,37 @@
 
     lower_half = iota((64, 128), 1) < 64
 
+    def finish(z, act):
+        act = jnp.maximum(act, 0.0).astype(BF16).reshape(6, 64, 256)
+        s_ref[z] = act[1:5]
+        full = act.astype(F32)
+        both = full[:, :, :128] + full[:, :, 128:]
+        for j in range(3):
+            even, odd = both[2 * j], both[2 * j + 1]
+            even = even + pltpu.roll(even, 64, 1)
+            odd = odd + pltpu.roll(odd, 64, 1)
+            q_ref[z, j] = jnp.where(lower_half, even, odd)
+
     def second_step(k, carry):
-        z = 4 * k
-        products = []
-        for w, (i, j) in enumerate(((0, 2), (1, 2), (2, 1), (1, 3))):
-            mixed = []
-            for p in range(2):
-                first, second = a_ref[z + 2 * p + i], a_ref[z + 2 * p + j]
-                mixed.append(first + second if w == 1 else first - second)
-            product = None
-            for y in range(4):
-                lhs = jnp.concatenate(
-                    [m[y % 2, y // 2 : y // 2 + 6].reshape(384, 256) for m in mixed], axis=0
-                )
-                at = 256 * (4 * w + y)
-                term = dot(lhs, w2_ref[at : at + 256, :])
-                product = term if product is None else product + term
-            products.append(product)
-        m0, m1, m2, m3 = products
-        acts = [m0 + m1 + m2, m1 - m2 - m3]
-        acts = [jnp.maximum(act, 0.0).astype(BF16).reshape(2, 6, 64, 256) for act in acts]
-        planes = [acts[d % 2][d // 2] for d in range(4)]
-        for d, plane in enumerate(planes):
-            s_ref[z + d] = plane[1:5]
-        for d, plane in enumerate(planes):
-            full = plane.astype(F32)
-            both = full[:, :, :128] + full[:, :, 128:]
-            for j in range(3):
-                even, odd = both[2 * j], both[2 * j + 1]
-                even = even + pltpu.roll(even, 64, 1)
-                odd = odd + pltpu.roll(odd, 64, 1)
-                q_ref[z + d, j] = jnp.where(lower_half, even, odd)
+        for p in range(5):
+            z = 10 * k + 2 * p
+            products = []
+            for w, (i, j) in enumerate(((0, 2), (1, 2), (2, 1), (1, 3))):
+                first, second = a_ref[z + i], a_ref[z + j]
+                mixed = first + second if w == 1 else first - second
+                product = None
+                for y in range(4):
+                    lhs = mixed[y % 2, y // 2 : y // 2 + 6].reshape(384, 256)
+                    at = 256 * (4 * w + y)
+                    term = dot(lhs, w2_ref[at : at + 256, :])
+                    product = term if product is None else product + term
+                products.append(product)
+            m0, m1, m2, m3 = products
+            finish(z, m0 + m1 + m2)
+            finish(z + 1, m1 - m2 - m3)
         return carry
 
-    lax.fori_loop(0, 5, second_step, 0)
+    lax.fori_loop(0, 2, second_step, 0)
 
     for z in range(2, 18, 4):
         logits = None

time: 26.1 us -> 25.4 us (0.973)
  Pallas kernels: 20.7 us -> 20 us
    pallas_call x1, Pallas kernels: 16.7 us -> 16.1 us  [local(): pl.pallas_call(body, out_shape=jax.ShapeDtypeStruct((3, 16, 8, 128), F32)...]
where the time goes in v3:
time: 25.4 us; the launch traced here: 25.3 us
  Pallas kernels  20 us (79%)
  starting transfers between devices  4.88 us (19%)
  waiting for transfers between devices  0.3 us (1%)
    pallas_call x1, Pallas kernels, local(): pl.pallas_call(body, out_shape=jax.ShapeDtypeStruct((3, 16, 8, 128), F32)...  16.1 us
    ppermute x1, starting transfers between devices, local(): ysides = [lax.ppermute(raw_volume, 'halo', neighbour_pairs(halo_count, 0))]  2.94 us
    pallas_call x1, Pallas kernels, local(): pl.pallas_call(prepare_second, out_shape=[jax.ShapeDtypeStruct((4096, 256...  2.29 us
    ppermute x1, starting transfers between devices, local(): lax.ppermute(jnp.where(odd, last_layers, first_layers), ('blocks', 'halo'...  1.87 us
    pallas_call x1, Pallas kernels, local(): pl.pallas_call(prepare_rest, out_shape=[jax.ShapeDtypeStruct((256, 1792),...  1.62 us
  transfers between devices with their start and end apart: 3, of which 1 were waited for; matrix products, arithmetic and copies ran while one was open for 0% of the time, Pallas kernels for 15%

profile of v3, /device:TPU:0, one launch (start us, length us, event | category | flops | bytes accessed | tf_op | source)
XLA Modules:
  0.0 25.3 jit_solution(16627620444271544241)
XLA Ops:
  0.0 2.9 %collective-permute-start = (bf16[16,8,128]{2,1,0:T(8,128)(2,1)}, bf16[16,8,128]{2,1,0:T(8,128)(2,1)S(1)}, u32[]{:S(2)}, u32[]{:S(2)}) collective-permute-start(bf16[16,8,128]{2,1,0:T(8,128)(2,1)} %raw_hbm.1), channel_id=1, source_target_pairs={{0,2},{2,0},{1,3},{3,1},{4,6},{6,4},{5,7},{7,5},{8,10},{10,8},{9,1... | collective-permute-start | bytes 98312 | tf_op jit(solution)/shard_map/ppermute | solution.py:347
  2.9 2.3 %shard_map.73 = (bf16[4096,256]{1,0:T(8,128)(2,1)S(1)}, bf16[1,3,3,3,64]{4,3,2,1,0:T(4,128)(2,1)S(1)}, bf16[27,4096]{1,0:T(8,128)(2,1)S(1)}, bf16[3,64]{1,0:T(4,128)(2,1)S(1)}, bf16[16,8,128]{2,1,0:T(8,128)(2,1)S(1)}) custom-call(bf16[1,3,3,3,64]{4,3,2,1,0:T(4,128)(2,1)} %bitcast.5, bf16[27,4096]{1,0:T(8,128)(2,1)} %second_hbm.1, ...), custom_call_target="tpu_custom_call" | custom-call | flops 1048576 | bytes 8388608 | tf_op jit(solution)/shard_map/pallas_call | solution.py:354
  5.2 0.0 collective-permute-done.refs_3_
  5.3 0.1 collective-permute-start.1
  5.4 1.9 %collective-permute-start.2 = (bf16[2,4,8,128]{3,2,1,0:T(8,128)(2,1)S(1)}, bf16[2,4,8,128]{3,2,1,0:T(8,128)(2,1)S(1)}, u32[]{:S(2)}, u32[]{:S(2)}) collective-permute-start(bf16[2,4,8,128]{3,2,1,0:T(8,128)(2,1)S(1)} %get-tuple-element.21), channel_id=1, source_target_pairs={{1,4},{4,1},{5,8},{8,5},{9,12},{12,9},{0,2},{13,15},{3,6},{6,3},{7... | collective-permute-start | bytes 49160 | tf_op jit(solution)/shard_map/ppermute | solution.py:373
  7.2 1.6 %shard_map.74 = (bf16[256,1792]{1,0:T(8,128)(2,1)S(1)}, bf16[3456,256]{1,0:T(8,128)(2,1)S(1)}, bf16[240,256]{1,0:T(8,128)(2,1)S(1)}) custom-call(bf16[1,3,3,3,64]{4,3,2,1,0:T(4,128)(2,1)S(1)} %get-tuple-element.14.first_ref, bf16[27,4096]{1,0:T(8,128)(2,1)S(1)} %get-tuple-element.15.coarse_ref, bf16[3,64]{1,0:T(4,128)(2,1)S(1)} %get-tuple-element.16.head_ref), custom_call_target="tpu_custom_call" | custom-call | flops 1048576 | bytes 6291456 | tf_op jit(solution)/shard_map/pallas_call | solution.py:379
  8.9 0.0 collective-permute-done.1.refs_4_
  8.9 0.3 %collective-permute-done.2.refs_5_ = bf16[2,4,8,128]{3,2,1,0:T(8,128)(2,1)S(1)} collective-permute-done((bf16[2,4,8,128]{3,2,1,0:T(8,128)(2,1)S(1)}, bf16[2,4,8,128]{3,2,1,0:T(8,128)(2,1)S(1)}, u32[]{:S(2)}, u32[]{:S(2)}) %collective-permute-start.2) | collective-permute-done | bytes 16416 | tf_op jit(solution)/shard_map/ppermute | solution.py:373
  9.2 16.1 %shard_map.75 = f32[3,16,8,128]{3,2,1,0:T(8,128)} custom-call(s32[1,1,4]{2,1,0:T(1,128)} %refs_0_.1, s32[1,1,4]{2,1,0:T(1,128)} %refs_1_.1, bf16[16,8,128]{2,1,0:T(8,128)(2,1)S(1)} %get-tuple-element.13.refs_2_, bf16[16,8,128]{2,1,0:T(8,128)(2,1)S(1)} %collective-permute-done.refs_3_, bf16[2,4,8,128]{3,2,1,0:T(8,128)(2,1)S(1)} %collective-permute-done.1.refs_4_, ...), custom_call_target="tpu_custom_call" | custom-call | flops 17179869184 | bytes 5242880 | tf_op jit(solution)/shard_map/pallas_call | solution.py:396
  (2 shorter events, 0.0 us)
Async XLA Ops:
  0.0 5.2 %collective-permute-start = (bf16[16,8,128]{2,1,0:T(8,128)(2,1)}, bf16[16,8,128]{2,1,0:T(8,128)(2,1)S(1)}, u32[]{:S(2)}, u32[]{:S(2)}) collective-permute-start(bf16[16,8,128]{2,1,0:T(8,128)(2,1)} %raw_hbm.1), channel_id=1, source_target_pairs={{0,2},{2,0},{1,3},{3,1},{4,6},{6,4},{5,7},{7,5},{8,10},{10,8},{9,1... | collective-permute-start | bytes 98312 | tf_op jit(solution)/shard_map/ppermute | solution.py:347
  5.3 3.6 %collective-permute-start.1 = (bf16[2,4,8,128]{3,2,1,0:T(8,128)(2,1)S(1)}, bf16[2,4,8,128]{3,2,1,0:T(8,128)(2,1)S(1)}, u32[]{:S(2)}, u32[]{:S(2)}) collective-permute-start(bf16[2,4,8,128]{3,2,1,0:T(8,128)(2,1)S(1)} %broadcast_select_fusion.1), channel_id=1, source_target_pairs={{0,1},{1,0},{2,3},{3,2},{4,5},{5,4},{6,7},{7,6},{8,9},{9,8},{10,11... | collective-permute-start | bytes 49160 | tf_op jit(solution)/shard_map/ppermute | solution.py:372
  5.4 3.8 %collective-permute-start.2 = (bf16[2,4,8,128]{3,2,1,0:T(8,128)(2,1)S(1)}, bf16[2,4,8,128]{3,2,1,0:T(8,128)(2,1)S(1)}, u32[]{:S(2)}, u32[]{:S(2)}) collective-permute-start(bf16[2,4,8,128]{3,2,1,0:T(8,128)(2,1)S(1)} %get-tuple-element.21), channel_id=1, source_target_pairs={{1,4},{4,1},{5,8},{8,5},{9,12},{12,9},{0,2},{13,15},{3,6},{6,3},{7... | collective-permute-start | bytes 49160 | tf_op jit(solution)/shard_map/ppermute | solution.py:373

commit v4 on v3

--- a/solution.py
+++ b/solution.py
@@ -160,6 +160,7 @@
 
     odd_h = halo_index % 2 == 1
     odd_g = gz_index == 1
+    once = jnp.minimum(tile_index + 1, 1)
 
     def with_rows(own, sides):
         own = own.astype(F32)
@@ -201,22 +202,21 @@
     keep_last = (edge_rows < 1) & (edge_lanes < 64)
 
     def first_step(k, carry):
-        z = 11 * k
-        lhs = u_ref[pl.ds(z, 11)].reshape(880, 256)
+        lhs = u_ref[...].reshape(1760, 256)
         for yp in range(7):
             res = jnp.maximum(dot(lhs, w1_ref[:, 256 * yp : 256 * (yp + 1)]), 0.0)
-            for d in range(11):
+            for d in range(22):
                 for yy in range(2):
                     tile = res[80 * d : 80 * d + 72, 128 * yy : 128 * (yy + 1)]
                     head = jnp.where(keep_first, tile[:8], 0.0)
                     tail = jnp.where(keep_last, tile[64:], 0.0)
                     tile = jnp.concatenate([head, tile[8:64], tail], axis=0)
-                    a_ref[z + d, yy, yp, :, 0:128] = tile[:64].astype(BF16)
+                    a_ref[d, yy, yp, :, 0:128] = tile[:64].astype(BF16)
                     after = pltpu.roll(tile, 71, 0)[:64]
-                    a_ref[z + d, yy, yp, :, 128:256] = after.astype(BF16)
+                    a_ref[d, yy, yp, :, 128:256] = after.astype(BF16)
         return carry
 
-    lax.fori_loop(0, 2, first_step, 0)
+    lax.fori_loop(0, once, first_step, 0)
 
     lower_half = iota((64, 128), 1) < 64
 
@@ -232,8 +232,8 @@
             q_ref[z, j] = jnp.where(lower_half, even, odd)
 
     def second_step(k, carry):
-        for p in range(5):
-            z = 10 * k + 2 * p
+        for p in range(10):
+            z = 2 * p
             products = []
             for w, (i, j) in enumerate(((0, 2), (1, 2), (2, 1), (1, 3))):
                 first, second = a_ref[z + i], a_ref[z + j]
@@ -250,7 +250,7 @@
             finish(z + 1, m1 - m2 - m3)
         return carry
 
-    lax.fori_loop(0, 2, second_step, 0)
+    second_step(0, 0)
 
     for z in range(2, 18, 4):
         logits = None

time: 25.4 us -> 24.9 us (0.980)
  Pallas kernels: 20 us -> 19.3 us
    pallas_call x1, Pallas kernels: 16.1 us -> 15.4 us  [local(): pl.pallas_call(body, out_shape=jax.ShapeDtypeStruct((3, 16, 8, 128), F32)...]
  transfers between devices with their start and end apart: 3 -> 3, of which waited for: 1 -> 1; matrix products, arithmetic and copies ran while one was open for 0% -> 0% of each run, Pallas kernels for 15% -> 16%
where the time goes in v4:
time: 24.9 us; the launch traced here: 24.7 us
  Pallas kernels  19.3 us (78%)
  starting transfers between devices  4.88 us (20%)
  waiting for transfers between devices  0.3 us (1%)
    pallas_call x1, Pallas kernels, local(): pl.pallas_call(body, out_shape=jax.ShapeDtypeStruct((3, 16, 8, 128), F32)...  15.4 us
    ppermute x1, starting transfers between devices, local(): ysides = [lax.ppermute(raw_volume, 'halo', neighbour_pairs(halo_count, 0))]  2.94 us
    pallas_call x1, Pallas kernels, local(): pl.pallas_call(prepare_second, out_shape=[jax.ShapeDtypeStruct((4096, 256...  2.29 us
    ppermute x1, starting transfers between devices, local(): lax.ppermute(jnp.where(odd, last_layers, first_layers), ('blocks', 'halo'...  1.87 us
    pallas_call x1, Pallas kernels, local(): pl.pallas_call(prepare_rest, out_shape=[jax.ShapeDtypeStruct((256, 1792),...  1.62 us
  transfers between devices with their start and end apart: 3, of which 1 were waited for; matrix products, arithmetic and copies ran while one was open for 0% of the time, Pallas kernels for 16%

profile of v4, /device:TPU:0, one launch (start us, length us, event | category | flops | bytes accessed | tf_op | source)
XLA Modules:
  0.0 24.7 jit_solution(14240207786585162719)
XLA Ops:
  0.0 2.9 %collective-permute-start = (bf16[16,8,128]{2,1,0:T(8,128)(2,1)}, bf16[16,8,128]{2,1,0:T(8,128)(2,1)S(1)}, u32[]{:S(2)}, u32[]{:S(2)}) collective-permute-start(bf16[16,8,128]{2,1,0:T(8,128)(2,1)} %raw_hbm.1), channel_id=1, source_target_pairs={{0,2},{2,0},{1,3},{3,1},{4,6},{6,4},{5,7},{7,5},{8,10},{10,8},{9,1... | collective-permute-start | bytes 98312 | tf_op jit(solution)/shard_map/ppermute | solution.py:347
  2.9 2.3 %shard_map.73 = (bf16[4096,256]{1,0:T(8,128)(2,1)S(1)}, bf16[1,3,3,3,64]{4,3,2,1,0:T(4,128)(2,1)S(1)}, bf16[27,4096]{1,0:T(8,128)(2,1)S(1)}, bf16[3,64]{1,0:T(4,128)(2,1)S(1)}, bf16[16,8,128]{2,1,0:T(8,128)(2,1)S(1)}) custom-call(bf16[1,3,3,3,64]{4,3,2,1,0:T(4,128)(2,1)} %bitcast.5, bf16[27,4096]{1,0:T(8,128)(2,1)} %second_hbm.1, ...), custom_call_target="tpu_custom_call" | custom-call | flops 1048576 | bytes 8388608 | tf_op jit(solution)/shard_map/pallas_call | solution.py:354
  5.2 0.0 collective-permute-done.refs_3_
  5.3 0.1 collective-permute-start.1
  5.4 1.9 %collective-permute-start.2 = (bf16[2,4,8,128]{3,2,1,0:T(8,128)(2,1)S(1)}, bf16[2,4,8,128]{3,2,1,0:T(8,128)(2,1)S(1)}, u32[]{:S(2)}, u32[]{:S(2)}) collective-permute-start(bf16[2,4,8,128]{3,2,1,0:T(8,128)(2,1)S(1)} %get-tuple-element.21), channel_id=1, source_target_pairs={{1,4},{4,1},{5,8},{8,5},{9,12},{12,9},{0,2},{13,15},{3,6},{6,3},{7... | collective-permute-start | bytes 49160 | tf_op jit(solution)/shard_map/ppermute | solution.py:373
  7.2 1.6 %shard_map.74 = (bf16[256,1792]{1,0:T(8,128)(2,1)S(1)}, bf16[3456,256]{1,0:T(8,128)(2,1)S(1)}, bf16[240,256]{1,0:T(8,128)(2,1)S(1)}) custom-call(bf16[1,3,3,3,64]{4,3,2,1,0:T(4,128)(2,1)S(1)} %get-tuple-element.14.first_ref, bf16[27,4096]{1,0:T(8,128)(2,1)S(1)} %get-tuple-element.15.coarse_ref, bf16[3,64]{1,0:T(4,128)(2,1)S(1)} %get-tuple-element.16.head_ref), custom_call_target="tpu_custom_call" | custom-call | flops 1048576 | bytes 6291456 | tf_op jit(solution)/shard_map/pallas_call | solution.py:379
  8.9 0.0 collective-permute-done.1.refs_4_
  8.9 0.3 %collective-permute-done.2.refs_5_ = bf16[2,4,8,128]{3,2,1,0:T(8,128)(2,1)S(1)} collective-permute-done((bf16[2,4,8,128]{3,2,1,0:T(8,128)(2,1)S(1)}, bf16[2,4,8,128]{3,2,1,0:T(8,128)(2,1)S(1)}, u32[]{:S(2)}, u32[]{:S(2)}) %collective-permute-start.2) | collective-permute-done | bytes 16416 | tf_op jit(solution)/shard_map/ppermute | solution.py:373
  9.2 15.4 %shard_map.75 = f32[3,16,8,128]{3,2,1,0:T(8,128)} custom-call(s32[1,1,4]{2,1,0:T(1,128)} %refs_0_.1, s32[1,1,4]{2,1,0:T(1,128)} %refs_1_.1, bf16[16,8,128]{2,1,0:T(8,128)(2,1)S(1)} %get-tuple-element.13.refs_2_, bf16[16,8,128]{2,1,0:T(8,128)(2,1)S(1)} %collective-permute-done.refs_3_, bf16[2,4,8,128]{3,2,1,0:T(8,128)(2,1)S(1)} %collective-permute-done.1.refs_4_, ...), custom_call_target="tpu_custom_call" | custom-call | flops 17179869184 | bytes 5242880 | tf_op jit(solution)/shard_map/pallas_call | solution.py:396
  (2 shorter events, 0.0 us)
Async XLA Ops:
  0.0 5.2 %collective-permute-start = (bf16[16,8,128]{2,1,0:T(8,128)(2,1)}, bf16[16,8,128]{2,1,0:T(8,128)(2,1)S(1)}, u32[]{:S(2)}, u32[]{:S(2)}) collective-permute-start(bf16[16,8,128]{2,1,0:T(8,128)(2,1)} %raw_hbm.1), channel_id=1, source_target_pairs={{0,2},{2,0},{1,3},{3,1},{4,6},{6,4},{5,7},{7,5},{8,10},{10,8},{9,1... | collective-permute-start | bytes 98312 | tf_op jit(solution)/shard_map/ppermute | solution.py:347
  5.3 3.6 %collective-permute-start.1 = (bf16[2,4,8,128]{3,2,1,0:T(8,128)(2,1)S(1)}, bf16[2,4,8,128]{3,2,1,0:T(8,128)(2,1)S(1)}, u32[]{:S(2)}, u32[]{:S(2)}) collective-permute-start(bf16[2,4,8,128]{3,2,1,0:T(8,128)(2,1)S(1)} %broadcast_select_fusion.1), channel_id=1, source_target_pairs={{0,1},{1,0},{2,3},{3,2},{4,5},{5,4},{6,7},{7,6},{8,9},{9,8},{10,11... | collective-permute-start | bytes 49160 | tf_op jit(solution)/shard_map/ppermute | solution.py:372
  5.4 3.8 %collective-permute-start.2 = (bf16[2,4,8,128]{3,2,1,0:T(8,128)(2,1)S(1)}, bf16[2,4,8,128]{3,2,1,0:T(8,128)(2,1)S(1)}, u32[]{:S(2)}, u32[]{:S(2)}) collective-permute-start(bf16[2,4,8,128]{3,2,1,0:T(8,128)(2,1)S(1)} %get-tuple-element.21), channel_id=1, source_target_pairs={{1,4},{4,1},{5,8},{8,5},{9,12},{12,9},{0,2},{13,15},{3,6},{6,3},{7... | collective-permute-start | bytes 49160 | tf_op jit(solution)/shard_map/ppermute | solution.py:373

commit v5 on v4

--- a/solution.py
+++ b/solution.py
@@ -218,6 +218,17 @@
 
     lax.fori_loop(0, once, first_step, 0)
 
+    for copy in copies:
+        copy.wait()
+    slots = counts_ref.shape[2]
+    total = jnp.int32(0)
+    anchors = [jnp.int32(0)] * MOST
+    for s in range(slots):
+        dense = counts_ref[0, 0, s] >= MINC
+        for j in range(MOST):
+            anchors[j] = jnp.where(dense & (total == j), offsets_ref[0, 0, s], anchors[j])
+        total = total + dense.astype(jnp.int32)
+
     lower_half = iota((64, 128), 1) < 64
 
     def finish(z, act):
@@ -259,17 +270,6 @@
             logits = term if logits is None else logits + term
         for d, plane in enumerate(side_by_side(logits)):
             fine_ref[z - 2 + d] = plane
-
-    for copy in copies:
-        copy.wait()
-    slots = counts_ref.shape[2]
-    total = jnp.int32(0)
-    anchors = [jnp.int32(0)] * MOST
-    for s in range(slots):
-        dense = counts_ref[0, 0, s] >= MINC
-        for j in range(MOST):
-            anchors[j] = jnp.where(dense & (total == j), offsets_ref[0, 0, s], anchors[j])
-        total = total + dense.astype(jnp.int32)
 
     rows64 = iota((64, 128), 0)
     for j in range(MOST):

time: 24.9 us -> 24.7 us (level)
  no operation moved by 1% of the time
where the time goes in v5:
time: 24.7 us; the launch traced here: 24.6 us
  Pallas kernels  19.2 us (78%)
  starting transfers between devices  4.88 us (20%)
  waiting for transfers between devices  0.3 us (1%)
    pallas_call x1, Pallas kernels, local(): pl.pallas_call(body, out_shape=jax.ShapeDtypeStruct((3, 16, 8, 128), F32)...  15.3 us
    ppermute x1, starting transfers between devices, local(): ysides = [lax.ppermute(raw_volume, 'halo', neighbour_pairs(halo_count, 0))]  2.94 us
    pallas_call x1, Pallas kernels, local(): pl.pallas_call(prepare_second, out_shape=[jax.ShapeDtypeStruct((4096, 256...  2.29 us
    ppermute x1, starting transfers between devices, local(): lax.ppermute(jnp.where(odd, last_layers, first_layers), ('blocks', 'halo'...  1.87 us
    pallas_call x1, Pallas kernels, local(): pl.pallas_call(prepare_rest, out_shape=[jax.ShapeDtypeStruct((256, 1792),...  1.62 us
  transfers between devices with their start and end apart: 3, of which 1 were waited for; matrix products, arithmetic and copies ran while one was open for 0% of the time, Pallas kernels for 16%

profile of v5, /device:TPU:0, one launch (start us, length us, event | category | flops | bytes accessed | tf_op | source)
XLA Modules:
  0.0 24.6 jit_solution(17000905288345430148)
XLA Ops:
  0.0 2.9 %collective-permute-start = (bf16[16,8,128]{2,1,0:T(8,128)(2,1)}, bf16[16,8,128]{2,1,0:T(8,128)(2,1)S(1)}, u32[]{:S(2)}, u32[]{:S(2)}) collective-permute-start(bf16[16,8,128]{2,1,0:T(8,128)(2,1)} %raw_hbm.1), channel_id=1, source_target_pairs={{0,2},{2,0},{1,3},{3,1},{4,6},{6,4},{5,7},{7,5},{8,10},{10,8},{9,1... | collective-permute-start | bytes 98312 | tf_op jit(solution)/shard_map/ppermute | solution.py:347
  2.9 2.3 %shard_map.73 = (bf16[4096,256]{1,0:T(8,128)(2,1)S(1)}, bf16[1,3,3,3,64]{4,3,2,1,0:T(4,128)(2,1)S(1)}, bf16[27,4096]{1,0:T(8,128)(2,1)S(1)}, bf16[3,64]{1,0:T(4,128)(2,1)S(1)}, bf16[16,8,128]{2,1,0:T(8,128)(2,1)S(1)}) custom-call(bf16[1,3,3,3,64]{4,3,2,1,0:T(4,128)(2,1)} %bitcast.5, bf16[27,4096]{1,0:T(8,128)(2,1)} %second_hbm.1, ...), custom_call_target="tpu_custom_call" | custom-call | flops 1048576 | bytes 8388608 | tf_op jit(solution)/shard_map/pallas_call | solution.py:354
  5.2 0.0 collective-permute-done.refs_3_
  5.3 0.1 collective-permute-start.1
  5.4 1.9 %collective-permute-start.2 = (bf16[2,4,8,128]{3,2,1,0:T(8,128)(2,1)S(1)}, bf16[2,4,8,128]{3,2,1,0:T(8,128)(2,1)S(1)}, u32[]{:S(2)}, u32[]{:S(2)}) collective-permute-start(bf16[2,4,8,128]{3,2,1,0:T(8,128)(2,1)S(1)} %get-tuple-element.21), channel_id=1, source_target_pairs={{1,4},{4,1},{5,8},{8,5},{9,12},{12,9},{0,2},{13,15},{3,6},{6,3},{7... | collective-permute-start | bytes 49160 | tf_op jit(solution)/shard_map/ppermute | solution.py:373
  7.2 1.6 %shard_map.74 = (bf16[256,1792]{1,0:T(8,128)(2,1)S(1)}, bf16[3456,256]{1,0:T(8,128)(2,1)S(1)}, bf16[240,256]{1,0:T(8,128)(2,1)S(1)}) custom-call(bf16[1,3,3,3,64]{4,3,2,1,0:T(4,128)(2,1)S(1)} %get-tuple-element.14.first_ref, bf16[27,4096]{1,0:T(8,128)(2,1)S(1)} %get-tuple-element.15.coarse_ref, bf16[3,64]{1,0:T(4,128)(2,1)S(1)} %get-tuple-element.16.head_ref), custom_call_target="tpu_custom_call" | custom-call | flops 1048576 | bytes 6291456 | tf_op jit(solution)/shard_map/pallas_call | solution.py:379
  8.9 0.0 collective-permute-done.1.refs_4_
  8.9 0.3 %collective-permute-done.2.refs_5_ = bf16[2,4,8,128]{3,2,1,0:T(8,128)(2,1)S(1)} collective-permute-done((bf16[2,4,8,128]{3,2,1,0:T(8,128)(2,1)S(1)}, bf16[2,4,8,128]{3,2,1,0:T(8,128)(2,1)S(1)}, u32[]{:S(2)}, u32[]{:S(2)}) %collective-permute-start.2) | collective-permute-done | bytes 16416 | tf_op jit(solution)/shard_map/ppermute | solution.py:373
  9.2 15.3 %shard_map.75 = f32[3,16,8,128]{3,2,1,0:T(8,128)} custom-call(s32[1,1,4]{2,1,0:T(1,128)} %refs_0_.1, s32[1,1,4]{2,1,0:T(1,128)} %refs_1_.1, bf16[16,8,128]{2,1,0:T(8,128)(2,1)S(1)} %get-tuple-element.13.refs_2_, bf16[16,8,128]{2,1,0:T(8,128)(2,1)S(1)} %collective-permute-done.refs_3_, bf16[2,4,8,128]{3,2,1,0:T(8,128)(2,1)S(1)} %collective-permute-done.1.refs_4_, ...), custom_call_target="tpu_custom_call" | custom-call | flops 17179869184 | bytes 5242880 | tf_op jit(solution)/shard_map/pallas_call | solution.py:396
  (2 shorter events, 0.0 us)
Async XLA Ops:
  0.0 5.2 %collective-permute-start = (bf16[16,8,128]{2,1,0:T(8,128)(2,1)}, bf16[16,8,128]{2,1,0:T(8,128)(2,1)S(1)}, u32[]{:S(2)}, u32[]{:S(2)}) collective-permute-start(bf16[16,8,128]{2,1,0:T(8,128)(2,1)} %raw_hbm.1), channel_id=1, source_target_pairs={{0,2},{2,0},{1,3},{3,1},{4,6},{6,4},{5,7},{7,5},{8,10},{10,8},{9,1... | collective-permute-start | bytes 98312 | tf_op jit(solution)/shard_map/ppermute | solution.py:347
  5.3 3.6 %collective-permute-start.1 = (bf16[2,4,8,128]{3,2,1,0:T(8,128)(2,1)S(1)}, bf16[2,4,8,128]{3,2,1,0:T(8,128)(2,1)S(1)}, u32[]{:S(2)}, u32[]{:S(2)}) collective-permute-start(bf16[2,4,8,128]{3,2,1,0:T(8,128)(2,1)S(1)} %broadcast_select_fusion.1), channel_id=1, source_target_pairs={{0,1},{1,0},{2,3},{3,2},{4,5},{5,4},{6,7},{7,6},{8,9},{9,8},{10,11... | collective-permute-start | bytes 49160 | tf_op jit(solution)/shard_map/ppermute | solution.py:372
  5.4 3.8 %collective-permute-start.2 = (bf16[2,4,8,128]{3,2,1,0:T(8,128)(2,1)S(1)}, bf16[2,4,8,128]{3,2,1,0:T(8,128)(2,1)S(1)}, u32[]{:S(2)}, u32[]{:S(2)}) collective-permute-start(bf16[2,4,8,128]{3,2,1,0:T(8,128)(2,1)S(1)} %get-tuple-element.21), channel_id=1, source_target_pairs={{1,4},{4,1},{5,8},{8,5},{9,12},{12,9},{0,2},{13,15},{3,6},{6,3},{7... | collective-permute-start | bytes 49160 | tf_op jit(solution)/shard_map/ppermute | solution.py:373

commit v6 on v5

--- a/solution.py
+++ b/solution.py
@@ -242,6 +242,14 @@
             odd = odd + pltpu.roll(odd, 64, 1)
             q_ref[z, j] = jnp.where(lower_half, even, odd)
 
+    def put_head(z):
+        logits = None
+        for yp in range(4):
+            term = dot_t(wh_ref[48 * yp : 48 * (yp + 1), :], s_ref[z : z + 4, yp].reshape(256, 256))
+            logits = term if logits is None else logits + term
+        for d, plane in enumerate(side_by_side(logits)):
+            fine_ref[z - 2 + d] = plane
+
     def second_step(k, carry):
         for p in range(10):
             z = 2 * p
@@ -259,17 +267,11 @@
             m0, m1, m2, m3 = products
             finish(z, m0 + m1 + m2)
             finish(z + 1, m1 - m2 - m3)
+            if p in (2, 4, 6, 8):
+                put_head(z - 2)
         return carry
 
     second_step(0, 0)
-
-    for z in range(2, 18, 4):
-        logits = None
-        for yp in range(4):
-            term = dot_t(wh_ref[48 * yp : 48 * (yp + 1), :], s_ref[z : z + 4, yp].reshape(256, 256))
-            logits = term if logits is None else logits + term
-        for d, plane in enumerate(side_by_side(logits)):
-            fine_ref[z - 2 + d] = plane
 
     rows64 = iota((64, 128), 0)
     for j in range(MOST):

time: 24.7 us -> 25.6 us (1.036)
  Pallas kernels: 19.2 us -> 20.1 us
    pallas_call x1, Pallas kernels: 15.3 us -> 16.1 us  [local(): pl.pallas_call(body, out_shape=jax.ShapeDtypeStruct((3, 16, 8, 128), F32)...]
  transfers between devices with their start and end apart: 3 -> 3, of which waited for: 1 -> 1; matrix products, arithmetic and copies ran while one was open for 0% -> 0% of each run, Pallas kernels for 16% -> 15%
where the time goes in v6:
time: 25.6 us; the launch traced here: 25.5 us
  Pallas kernels  20.1 us (79%)
  starting transfers between devices  4.88 us (19%)
  waiting for transfers between devices  0.3 us (1%)
    pallas_call x1, Pallas kernels, local(): pl.pallas_call(body, out_shape=jax.ShapeDtypeStruct((3, 16, 8, 128), F32)...  16.1 us
    ppermute x1, starting transfers between devices, local(): ysides = [lax.ppermute(raw_volume, 'halo', neighbour_pairs(halo_count, 0))]  2.94 us
    pallas_call x1, Pallas kernels, local(): pl.pallas_call(prepare_second, out_shape=[jax.ShapeDtypeStruct((4096, 256...  2.29 us
    ppermute x1, starting transfers between devices, local(): lax.ppermute(jnp.where(odd, last_layers, first_layers), ('blocks', 'halo'...  1.87 us
    pallas_call x1, Pallas kernels, local(): pl.pallas_call(prepare_rest, out_shape=[jax.ShapeDtypeStruct((256, 1792),...  1.62 us
  transfers between devices with their start and end apart: 3, of which 1 were waited for; matrix products, arithmetic and copies ran while one was open for 0% of the time, Pallas kernels for 15%

profile of v6, /device:TPU:0, one launch (start us, length us, event | category | flops | bytes accessed | tf_op | source)
XLA Modules:
  0.0 25.5 jit_solution(15656827030798775237)
XLA Ops:
  0.0 2.9 %collective-permute-start = (bf16[16,8,128]{2,1,0:T(8,128)(2,1)}, bf16[16,8,128]{2,1,0:T(8,128)(2,1)S(1)}, u32[]{:S(2)}, u32[]{:S(2)}) collective-permute-start(bf16[16,8,128]{2,1,0:T(8,128)(2,1)} %raw_hbm.1), channel_id=1, source_target_pairs={{0,2},{2,0},{1,3},{3,1},{4,6},{6,4},{5,7},{7,5},{8,10},{10,8},{9,1... | collective-permute-start | bytes 98312 | tf_op jit(solution)/shard_map/ppermute | solution.py:349
  2.9 2.3 %shard_map.73 = (bf16[4096,256]{1,0:T(8,128)(2,1)S(1)}, bf16[1,3,3,3,64]{4,3,2,1,0:T(4,128)(2,1)S(1)}, bf16[27,4096]{1,0:T(8,128)(2,1)S(1)}, bf16[3,64]{1,0:T(4,128)(2,1)S(1)}, bf16[16,8,128]{2,1,0:T(8,128)(2,1)S(1)}) custom-call(bf16[1,3,3,3,64]{4,3,2,1,0:T(4,128)(2,1)} %bitcast.5, bf16[27,4096]{1,0:T(8,128)(2,1)} %second_hbm.1, ...), custom_call_target="tpu_custom_call" | custom-call | flops 1048576 | bytes 8388608 | tf_op jit(solution)/shard_map/pallas_call | solution.py:356
  5.2 0.0 collective-permute-done.refs_3_
  5.3 0.1 collective-permute-start.1
  5.4 1.9 %collective-permute-start.2 = (bf16[2,4,8,128]{3,2,1,0:T(8,128)(2,1)S(1)}, bf16[2,4,8,128]{3,2,1,0:T(8,128)(2,1)S(1)}, u32[]{:S(2)}, u32[]{:S(2)}) collective-permute-start(bf16[2,4,8,128]{3,2,1,0:T(8,128)(2,1)S(1)} %get-tuple-element.21), channel_id=1, source_target_pairs={{1,4},{4,1},{5,8},{8,5},{9,12},{12,9},{0,2},{13,15},{3,6},{6,3},{7... | collective-permute-start | bytes 49160 | tf_op jit(solution)/shard_map/ppermute | solution.py:375
  7.2 1.6 %shard_map.74 = (bf16[256,1792]{1,0:T(8,128)(2,1)S(1)}, bf16[3456,256]{1,0:T(8,128)(2,1)S(1)}, bf16[240,256]{1,0:T(8,128)(2,1)S(1)}) custom-call(bf16[1,3,3,3,64]{4,3,2,1,0:T(4,128)(2,1)S(1)} %get-tuple-element.14.first_ref, bf16[27,4096]{1,0:T(8,128)(2,1)S(1)} %get-tuple-element.15.coarse_ref, bf16[3,64]{1,0:T(4,128)(2,1)S(1)} %get-tuple-element.16.head_ref), custom_call_target="tpu_custom_call" | custom-call | flops 1048576 | bytes 6291456 | tf_op jit(solution)/shard_map/pallas_call | solution.py:381
  8.9 0.0 collective-permute-done.1.refs_4_
  8.9 0.3 %collective-permute-done.2.refs_5_ = bf16[2,4,8,128]{3,2,1,0:T(8,128)(2,1)S(1)} collective-permute-done((bf16[2,4,8,128]{3,2,1,0:T(8,128)(2,1)S(1)}, bf16[2,4,8,128]{3,2,1,0:T(8,128)(2,1)S(1)}, u32[]{:S(2)}, u32[]{:S(2)}) %collective-permute-start.2) | collective-permute-done | bytes 16416 | tf_op jit(solution)/shard_map/ppermute | solution.py:375
  9.2 16.1 %shard_map.75 = f32[3,16,8,128]{3,2,1,0:T(8,128)} custom-call(s32[1,1,4]{2,1,0:T(1,128)} %refs_0_.1, s32[1,1,4]{2,1,0:T(1,128)} %refs_1_.1, bf16[16,8,128]{2,1,0:T(8,128)(2,1)S(1)} %get-tuple-element.13.refs_2_, bf16[16,8,128]{2,1,0:T(8,128)(2,1)S(1)} %collective-permute-done.refs_3_, bf16[2,4,8,128]{3,2,1,0:T(8,128)(2,1)S(1)} %collective-permute-done.1.refs_4_, ...), custom_call_target="tpu_custom_call" | custom-call | flops 17179869184 | bytes 5242880 | tf_op jit(solution)/shard_map/pallas_call | solution.py:398
  (2 shorter events, 0.0 us)
Async XLA Ops:
  0.0 5.2 %collective-permute-start = (bf16[16,8,128]{2,1,0:T(8,128)(2,1)}, bf16[16,8,128]{2,1,0:T(8,128)(2,1)S(1)}, u32[]{:S(2)}, u32[]{:S(2)}) collective-permute-start(bf16[16,8,128]{2,1,0:T(8,128)(2,1)} %raw_hbm.1), channel_id=1, source_target_pairs={{0,2},{2,0},{1,3},{3,1},{4,6},{6,4},{5,7},{7,5},{8,10},{10,8},{9,1... | collective-permute-start | bytes 98312 | tf_op jit(solution)/shard_map/ppermute | solution.py:349
  5.3 3.6 %collective-permute-start.1 = (bf16[2,4,8,128]{3,2,1,0:T(8,128)(2,1)S(1)}, bf16[2,4,8,128]{3,2,1,0:T(8,128)(2,1)S(1)}, u32[]{:S(2)}, u32[]{:S(2)}) collective-permute-start(bf16[2,4,8,128]{3,2,1,0:T(8,128)(2,1)S(1)} %broadcast_select_fusion.1), channel_id=1, source_target_pairs={{0,1},{1,0},{2,3},{3,2},{4,5},{5,4},{6,7},{7,6},{8,9},{9,8},{10,11... | collective-permute-start | bytes 49160 | tf_op jit(solution)/shard_map/ppermute | solution.py:374
  5.4 3.8 %collective-permute-start.2 = (bf16[2,4,8,128]{3,2,1,0:T(8,128)(2,1)S(1)}, bf16[2,4,8,128]{3,2,1,0:T(8,128)(2,1)S(1)}, u32[]{:S(2)}, u32[]{:S(2)}) collective-permute-start(bf16[2,4,8,128]{3,2,1,0:T(8,128)(2,1)S(1)} %get-tuple-element.21), channel_id=1, source_target_pairs={{1,4},{4,1},{5,8},{8,5},{9,12},{12,9},{0,2},{13,15},{3,6},{6,3},{7... | collective-permute-start | bytes 49160 | tf_op jit(solution)/shard_map/ppermute | solution.py:375
